TPU v7x, 128 devices: a whole 4x4x4 slice. The times are simulated.
128 devices in a mesh: tables: 16 (over y, x), replica: 8 (over z, core).
Axes of the slice: x: 4, y: 4, z: 4, core: 2. Of those that a mesh axis runs over, the one named last changes fastest.
Arguments:
- core_first: bfloat16 [16, 512, 512], P('tables'), may hold values from -6 to 6
- core_middle: bfloat16 [16, 80, 64, 128], P('tables'), may hold values from -0.75 to 0.75
- core_last: bfloat16 [16, 512, 512], P('tables'), may hold values from -0.75 to 0.75
- idx_first: int32 [8, 16, 320, 16, 2], P('replica', 'tables'), may hold values from 0 to 511
- idx_middle: int32 [8, 16, 320, 16, 2], P('replica', 'tables'), may hold values from 0 to 79
- idx_last: int32 [8, 16, 320, 16, 2], P('replica', 'tables'), may hold values from 0 to 511
- bag_lengths: int32 [8, 16, 320, 16], P('replica', 'tables'), may hold values from 1 to 2
- cross_down: bfloat16 [2, 2048, 256], replicated, may hold values from -0.0625 to 0.0625
- cross_up: bfloat16 [2, 256, 2048], replicated, may hold values from -0.1875 to 0.1875
- cross_bias: bfloat16 [2, 2048], replicated, may hold values from -3 to 3
- top_weight: bfloat16 [2048, 4096], P(None, 'tables'), may hold values from -0.125 to 0.125
- top_bias: bfloat16 [4096], replicated, may hold values from -3 to 3
- out_weight: bfloat16 [4096], replicated, may hold values from -0.09375 to 0.09375
- prior: float32 [8, 16, 320], P('replica', 'tables'), may hold values from -4.5 to 4.5
Outputs:
- logits: float32 [8, 16, 320], P('replica', 'tables')
- click_share: float32 [8, 16, 320], P('replica', 'tables')
All inputs are finite; a program needn't handle non-finite values.
Results may differ from a plain program's by a relative error of at most 0.0035.
Values may be sent and summed in bfloat16 or wider, within the bound.
A program may use at most 128 MiB of HBM per device.

v0:
```python
import jax
import jax.numpy as jnp
from jax import lax
from jax.sharding import PartitionSpec as P

D1 = 8
D2 = 2
D3 = 8
BAG = 2


def rows_of(first_core, middle_core, last_core, first_ids, middle_ids, last_ids):
    item_count = first_ids.shape[0]
    rank_size = middle_core.shape[1]
    first_rows = first_core[first_ids].reshape(item_count, -1, rank_size)
    middle_rows = middle_core[middle_ids]
    left_part = jnp.einsum(
        "kdr,krm->kdm", first_rows, middle_rows, preferred_element_type=jnp.float32
    ).astype(jnp.bfloat16)
    left_part = left_part.reshape(item_count, D1 * D2, rank_size)
    last_rows = last_core[last_ids].reshape(item_count, rank_size, D3)
    return jnp.einsum(
        "kar,krd->kad", left_part, last_rows, preferred_element_type=jnp.float32
    ).reshape(item_count, D1 * D2 * D3)


def pool_owned(core_first, core_middle, core_last, received, shards):
    first_ids, middle_ids, last_ids, lengths = received

    def pooled_block(block_ids):
        first_block, middle_block, last_block, length_block = block_ids
        rows_here = first_block.shape[0]
        in_bag = (
            jnp.arange(BAG, dtype=jnp.int32)[None, None, :] < length_block[:, :, None]
        ).astype(jnp.float32)
        row_vecs = rows_of(
            core_first[0],
            core_middle[0],
            core_last[0],
            first_block[:, 0].reshape(-1),
            middle_block[:, 0].reshape(-1),
            last_block[:, 0].reshape(-1),
        )
        row_vecs = row_vecs.reshape(rows_here, BAG, D1 * D2 * D3)
        columns = [jnp.sum(row_vecs * in_bag[:, 0, :, None], axis=1)]
        return jnp.stack(columns, axis=1)

    def blocked(values):
        return values.reshape((shards, -1) + values.shape[2:])

    pooled = lax.map(
        pooled_block, (blocked(first_ids), blocked(middle_ids), blocked(last_ids), blocked(lengths))
    )
    return pooled.reshape((-1, 1) + pooled.shape[2:])


def body(
    core_first,
    core_middle,
    core_last,
    idx_first,
    idx_middle,
    idx_last,
    bag_lengths,
    cross_down,
    cross_up,
    cross_bias,
    top_weight,
    top_bias,
    out_weight,
    prior,
):
    shards = lax.axis_size("tables")
    replicas = lax.axis_size("replica")
    queries = idx_first.shape[2]
    tab_dev = core_first.shape[0]

    def by_owner(values):
        return values.reshape((queries, shards, tab_dev) + values.shape[2:])

    first_ids = by_owner(idx_first[0, 0])
    middle_ids = by_owner(idx_middle[0, 0])
    last_ids = by_owner(idx_last[0, 0])
    lengths = by_owner(bag_lengths[0, 0])
    at_owner = (
        lax.all_to_all(first_ids, "tables", split_axis=1, concat_axis=0, tiled=True),
        lax.all_to_all(middle_ids, "tables", split_axis=1, concat_axis=0, tiled=True),
        lax.all_to_all(last_ids, "tables", split_axis=1, concat_axis=0, tiled=True),
        lax.all_to_all(lengths, "tables", split_axis=1, concat_axis=0, tiled=True),
    )
    pooled = pool_owned(core_first, core_middle, core_last, at_owner, shards)
    returned = lax.all_to_all(pooled, "tables", split_axis=0, concat_axis=1, tiled=True)
    features = returned.reshape(queries, -1)
    crossed = features
    for layer_pos in range(cross_down.shape[0]):
        low_rank = jnp.dot(
            crossed.astype(jnp.bfloat16), cross_down[layer_pos], preferred_element_type=jnp.float32
        ).astype(jnp.bfloat16)
        lifted = jnp.dot(low_rank, cross_up[layer_pos], preferred_element_type=jnp.float32)
        crossed = features * (lifted + cross_bias[layer_pos].astype(jnp.float32)) + crossed
    crossed_low = crossed.astype(jnp.bfloat16)
    hid_dev = top_weight.shape[1]
    offset = lax.axis_index("tables") * hid_dev
    bias_part = lax.dynamic_slice_in_dim(top_bias, offset, hid_dev).astype(jnp.float32)
    out_part = lax.dynamic_slice_in_dim(out_weight, offset, hid_dev)
    hidden = jax.nn.relu(
        jnp.dot(
            lax.all_gather(crossed_low, "tables", axis=0, tiled=True),
            top_weight,
            preferred_element_type=jnp.float32,
        )
        + bias_part
    ).astype(jnp.bfloat16)
    partial_logits = jnp.dot(hidden, out_part, preferred_element_type=jnp.float32)
    summed = lax.psum_scatter(partial_logits, "tables", scatter_dimension=0, tiled=True)
    logits = summed + prior[0, 0]
    clicks = jax.nn.sigmoid(logits)
    request_sum = lax.psum(jnp.sum(clicks), "replica")
    click_share = replicas * queries * clicks / request_sum
    return (logits[None, None], click_share[None, None])


def solution(mesh):
    in_specs = (
        P("tables", None, None),
        P("tables", None, None, None),
        P("tables", None, None),
        P("replica", "tables", None, None, None),
        P("replica", "tables", None, None, None),
        P("replica", "tables", None, None, None),
        P("replica", "tables", None, None),
        P(),
        P(),
        P(),
        P(None, "tables"),
        P(),
        P(),
        P("replica", "tables", None),
    )
    out_specs = (P("replica", "tables", None), P("replica", "tables", None))
    return jax.shard_map(body, mesh=mesh, in_specs=in_specs, out_specs=out_specs, check_vma=False)
```

profile of v0, /device:TPU:1, one launch (start us, length us, event | category | flops | bytes accessed | tf_op | source)
XLA Modules:
  0.0 1251.9 jit_solution(17001115150761433571)
XLA Ops:
  8.0 13.8 %all_to_all.75 = s32[320,16,1]{0,2,1:T(1,128)S(1)} all-to-all(s32[320,16,1]{0,2,1:T(1,128)S(1)} %reshape_squeeze.15), channel_id=1, replica_groups=mesh['tables'=16,'replica'=8] {'tables'}, dimensions={1} | all-to-all | bytes 40960 | tf_op jit(solution)/shard_map/all_to_all | solution.py:89
  21.9 9.9 all_to_all.76
  31.7 9.9 all_to_all.77
  51.5 902.2 %while.10 = (s32[]{:T(128)}, f32[16,320,1,128]{3,2,1,0:T(1,128)}, bf16[1,512,512]{2,1,0:T(8,128)(2,1)}, s32[16,320,1,2]{1,3,0,2:T(2,128)S(1)}, bf16[1,80,64,128]...) while((s32[]{:T(128)}, f32[16,320,1,128]{3,2,1,0:T(1,128)}, ...), condition=%wide.region_2.3_spmd, body=%wide.region_0.2_spmd.sunk | while | flops 95160192 | bytes 54591912 | solution.py:51
  51.9 21.0 %gather_fusion.1 = bf16[640,64,128]{2,1,0:T(8,128)(2,1)} fusion(bf16[80,64,128]{2,1,0:T(8,128)(2,1)} %bitcast.113, s32[1024]{0:T(1024)S(1)} %pad_clamp_fusion.7), kind=kCustom, calls=%fused_computation.1.clone.1 | custom fusion | bytes 20974080 | tf_op jit(solution)/shard_map/while/body/eval_jaxpr/gather | solution.py:16
  78.2 7.2 convolution_convert_fusion.2
  108.3 21.0 %gather_fusion.1 = bf16[640,64,128]{2,1,0:T(8,128)(2,1)} fusion(bf16[80,64,128]{2,1,0:T(8,128)(2,1)} %bitcast.113, s32[1024]{0:T(1024)S(1)} %pad_clamp_fusion.7), kind=kCustom, calls=%fused_computation.1.clone.1 | custom fusion | bytes 20974080 | tf_op jit(solution)/shard_map/while/body/eval_jaxpr/gather | solution.py:16
  134.6 7.2 convolution_convert_fusion.2
  164.7 21.0 %gather_fusion.1 = bf16[640,64,128]{2,1,0:T(8,128)(2,1)} fusion(bf16[80,64,128]{2,1,0:T(8,128)(2,1)} %bitcast.113, s32[1024]{0:T(1024)S(1)} %pad_clamp_fusion.7), kind=kCustom, calls=%fused_computation.1.clone.1 | custom fusion | bytes 20974080 | tf_op jit(solution)/shard_map/while/body/eval_jaxpr/gather | solution.py:16
  191.0 7.2 convolution_convert_fusion.2
  221.0 21.0 %gather_fusion.1 = bf16[640,64,128]{2,1,0:T(8,128)(2,1)} fusion(bf16[80,64,128]{2,1,0:T(8,128)(2,1)} %bitcast.113, s32[1024]{0:T(1024)S(1)} %pad_clamp_fusion.7), kind=kCustom, calls=%fused_computation.1.clone.1 | custom fusion | bytes 20974080 | tf_op jit(solution)/shard_map/while/body/eval_jaxpr/gather | solution.py:16
  247.4 7.2 convolution_convert_fusion.2
  277.4 21.0 %gather_fusion.1 = bf16[640,64,128]{2,1,0:T(8,128)(2,1)} fusion(bf16[80,64,128]{2,1,0:T(8,128)(2,1)} %bitcast.113, s32[1024]{0:T(1024)S(1)} %pad_clamp_fusion.7), kind=kCustom, calls=%fused_computation.1.clone.1 | custom fusion | bytes 20974080 | tf_op jit(solution)/shard_map/while/body/eval_jaxpr/gather | solution.py:16
  303.8 7.2 convolution_convert_fusion.2
  333.8 21.0 %gather_fusion.1 = bf16[640,64,128]{2,1,0:T(8,128)(2,1)} fusion(bf16[80,64,128]{2,1,0:T(8,128)(2,1)} %bitcast.113, s32[1024]{0:T(1024)S(1)} %pad_clamp_fusion.7), kind=kCustom, calls=%fused_computation.1.clone.1 | custom fusion | bytes 20974080 | tf_op jit(solution)/shard_map/while/body/eval_jaxpr/gather | solution.py:16
  360.2 7.2 convolution_convert_fusion.2
  390.2 21.0 %gather_fusion.1 = bf16[640,64,128]{2,1,0:T(8,128)(2,1)} fusion(bf16[80,64,128]{2,1,0:T(8,128)(2,1)} %bitcast.113, s32[1024]{0:T(1024)S(1)} %pad_clamp_fusion.7), kind=kCustom, calls=%fused_computation.1.clone.1 | custom fusion | bytes 20974080 | tf_op jit(solution)/shard_map/while/body/eval_jaxpr/gather | solution.py:16
  416.5 7.2 convolution_convert_fusion.2
  446.6 21.0 %gather_fusion.1 = bf16[640,64,128]{2,1,0:T(8,128)(2,1)} fusion(bf16[80,64,128]{2,1,0:T(8,128)(2,1)} %bitcast.113, s32[1024]{0:T(1024)S(1)} %pad_clamp_fusion.7), kind=kCustom, calls=%fused_computation.1.clone.1 | custom fusion | bytes 20974080 | tf_op jit(solution)/shard_map/while/body/eval_jaxpr/gather | solution.py:16
  503.0 21.0 %gather_fusion.1 = bf16[640,64,128]{2,1,0:T(8,128)(2,1)} fusion(bf16[80,64,128]{2,1,0:T(8,128)(2,1)} %bitcast.113, s32[1024]{0:T(1024)S(1)} %pad_clamp_fusion.7), kind=kCustom, calls=%fused_computation.1.clone.1 | custom fusion | bytes 20974080 | tf_op jit(solution)/shard_map/while/body/eval_jaxpr/gather | solution.py:16
  559.4 21.0 %gather_fusion.1 = bf16[640,64,128]{2,1,0:T(8,128)(2,1)} fusion(bf16[80,64,128]{2,1,0:T(8,128)(2,1)} %bitcast.113, s32[1024]{0:T(1024)S(1)} %pad_clamp_fusion.7), kind=kCustom, calls=%fused_computation.1.clone.1 | custom fusion | bytes 20974080 | tf_op jit(solution)/shard_map/while/body/eval_jaxpr/gather | solution.py:16
  615.8 21.0 %gather_fusion.1 = bf16[640,64,128]{2,1,0:T(8,128)(2,1)} fusion(bf16[80,64,128]{2,1,0:T(8,128)(2,1)} %bitcast.113, s32[1024]{0:T(1024)S(1)} %pad_clamp_fusion.7), kind=kCustom, calls=%fused_computation.1.clone.1 | custom fusion | bytes 20974080 | tf_op jit(solution)/shard_map/while/body/eval_jaxpr/gather | solution.py:16
  672.1 21.0 %gather_fusion.1 = bf16[640,64,128]{2,1,0:T(8,128)(2,1)} fusion(bf16[80,64,128]{2,1,0:T(8,128)(2,1)} %bitcast.113, s32[1024]{0:T(1024)S(1)} %pad_clamp_fusion.7), kind=kCustom, calls=%fused_computation.1.clone.1 | custom fusion | bytes 20974080 | tf_op jit(solution)/shard_map/while/body/eval_jaxpr/gather | solution.py:16
  728.5 21.0 %gather_fusion.1 = bf16[640,64,128]{2,1,0:T(8,128)(2,1)} fusion(bf16[80,64,128]{2,1,0:T(8,128)(2,1)} %bitcast.113, s32[1024]{0:T(1024)S(1)} %pad_clamp_fusion.7), kind=kCustom, calls=%fused_computation.1.clone.1 | custom fusion | bytes 20974080 | tf_op jit(solution)/shard_map/while/body/eval_jaxpr/gather | solution.py:16
  784.9 21.0 %gather_fusion.1 = bf16[640,64,128]{2,1,0:T(8,128)(2,1)} fusion(bf16[80,64,128]{2,1,0:T(8,128)(2,1)} %bitcast.113, s32[1024]{0:T(1024)S(1)} %pad_clamp_fusion.7), kind=kCustom, calls=%fused_computation.1.clone.1 | custom fusion | bytes 20974080 | tf_op jit(solution)/shard_map/while/body/eval_jaxpr/gather | solution.py:16
  841.3 21.0 %gather_fusion.1 = bf16[640,64,128]{2,1,0:T(8,128)(2,1)} fusion(bf16[80,64,128]{2,1,0:T(8,128)(2,1)} %bitcast.113, s32[1024]{0:T(1024)S(1)} %pad_clamp_fusion.7), kind=kCustom, calls=%fused_computation.1.clone.1 | custom fusion | bytes 20974080 | tf_op jit(solution)/shard_map/while/body/eval_jaxpr/gather | solution.py:16
  897.7 21.0 %gather_fusion.1 = bf16[640,64,128]{2,1,0:T(8,128)(2,1)} fusion(bf16[80,64,128]{2,1,0:T(8,128)(2,1)} %bitcast.113, s32[1024]{0:T(1024)S(1)} %pad_clamp_fusion.7), kind=kCustom, calls=%fused_computation.1.clone.1 | custom fusion | bytes 20974080 | tf_op jit(solution)/shard_map/while/body/eval_jaxpr/gather | solution.py:16
  958.4 30.1 %all-to-all-done.4 = f32[5120,1,1,128]{3,2,1,0:T(1,128)} async-done(((f32[5120,1,1,128]{3,2,1,0:T(1,128)}), f32[5120,1,1,128]{3,2,1,0:T(1,128)}, u32[]{:S(2)}, u32[]{:S(2)}) %all-to-all-start.4) | async-done | bytes 2621472 | tf_op jit(solution)/shard_map/all_to_all | solution.py:92
  1011.4 135.0 %all-gather.2.cloned.1.call-done = bf16[5120,2048]{1,0:T(8,128)(2,1)} async-done(((bf16[320,2048]{1,0:T(8,128)(2,1)}), bf16[5120,2048]{1,0:T(8,128)(2,1)}) %all-gather.2.cloned.1.call-update) | async-done | bytes 20971536 | tf_op jit(solution)/shard_map/all_gather | solution.py:108
  1146.4 10.6 fusion.36
  1157.0 58.5 %all-reduce = f32[5120]{0:T(1024)S(1)} all-reduce(f32[5120]{0:T(1024)S(1)} %bitcast.133), channel_id=2, replica_groups=mesh['tables'=16,'replica'=8] {'tables'}, use_global_device_ids=true, to_apply=%region_3.4.clone | all-reduce | flops 5120 | bytes 40960
  1216.2 27.1 %psum.7 = f32[]{:T(128)} all-reduce(f32[]{:T(128)} %get-tuple-element.77), channel_id=1, replica_groups=mesh['tables'=16,'replica'=8] {'replica'}, use_global_device_ids=true, to_apply=%region_5.6 | all-reduce | flops 1 | bytes 8 | tf_op jit(solution)/shard_map/psum | solution.py:118
  (551 shorter events, 552.7 us)
Async XLA Ops:
  7.2 1139.2 %copy-start = (bf16[2048,256]{1,0:T(8,128)(2,1)S(1)}, bf16[2048,256]{1,0:T(8,128)(2,1)}, u32[]{:S(2)}) copy-start(bf16[2048,256]{1,0:T(8,128)(2,1)} %param.26) | copy-start | bytes 3145732
  41.6 9.9 all-to-all-start.2
  51.9 21.4 %copy-start.1 = (bf16[1,512,512]{2,1,0:T(8,128)(2,1)S(1)}, bf16[1,512,512]{2,1,0:T(8,128)(2,1)}, u32[]{:S(2)}) copy-start(bf16[1,512,512]{2,1,0:T(8,128)(2,1)} %get-tuple-element.164) | copy-start | bytes 1572868 | tf_op jit(solution)/shard_map/while
  87.4 5.2 copy-start.2
  108.3 21.4 %copy-start.1 = (bf16[1,512,512]{2,1,0:T(8,128)(2,1)S(1)}, bf16[1,512,512]{2,1,0:T(8,128)(2,1)}, u32[]{:S(2)}) copy-start(bf16[1,512,512]{2,1,0:T(8,128)(2,1)} %get-tuple-element.164) | copy-start | bytes 1572868 | tf_op jit(solution)/shard_map/while
  143.8 5.2 copy-start.2
  164.7 21.4 %copy-start.1 = (bf16[1,512,512]{2,1,0:T(8,128)(2,1)S(1)}, bf16[1,512,512]{2,1,0:T(8,128)(2,1)}, u32[]{:S(2)}) copy-start(bf16[1,512,512]{2,1,0:T(8,128)(2,1)} %get-tuple-element.164) | copy-start | bytes 1572868 | tf_op jit(solution)/shard_map/while
  221.0 21.4 %copy-start.1 = (bf16[1,512,512]{2,1,0:T(8,128)(2,1)S(1)}, bf16[1,512,512]{2,1,0:T(8,128)(2,1)}, u32[]{:S(2)}) copy-start(bf16[1,512,512]{2,1,0:T(8,128)(2,1)} %get-tuple-element.164) | copy-start | bytes 1572868 | tf_op jit(solution)/shard_map/while
  256.6 5.2 copy-start.2
  277.4 21.4 %copy-start.1 = (bf16[1,512,512]{2,1,0:T(8,128)(2,1)S(1)}, bf16[1,512,512]{2,1,0:T(8,128)(2,1)}, u32[]{:S(2)}) copy-start(bf16[1,512,512]{2,1,0:T(8,128)(2,1)} %get-tuple-element.164) | copy-start | bytes 1572868 | tf_op jit(solution)/shard_map/while
  333.8 21.4 %copy-start.1 = (bf16[1,512,512]{2,1,0:T(8,128)(2,1)S(1)}, bf16[1,512,512]{2,1,0:T(8,128)(2,1)}, u32[]{:S(2)}) copy-start(bf16[1,512,512]{2,1,0:T(8,128)(2,1)} %get-tuple-element.164) | copy-start | bytes 1572868 | tf_op jit(solution)/shard_map/while
  390.2 21.4 %copy-start.1 = (bf16[1,512,512]{2,1,0:T(8,128)(2,1)S(1)}, bf16[1,512,512]{2,1,0:T(8,128)(2,1)}, u32[]{:S(2)}) copy-start(bf16[1,512,512]{2,1,0:T(8,128)(2,1)} %get-tuple-element.164) | copy-start | bytes 1572868 | tf_op jit(solution)/shard_map/while
  425.7 5.2 copy-start.2
  446.6 21.4 %copy-start.1 = (bf16[1,512,512]{2,1,0:T(8,128)(2,1)S(1)}, bf16[1,512,512]{2,1,0:T(8,128)(2,1)}, u32[]{:S(2)}) copy-start(bf16[1,512,512]{2,1,0:T(8,128)(2,1)} %get-tuple-element.164) | copy-start | bytes 1572868 | tf_op jit(solution)/shard_map/while
  482.1 5.2 copy-start.2
  503.0 21.4 %copy-start.1 = (bf16[1,512,512]{2,1,0:T(8,128)(2,1)S(1)}, bf16[1,512,512]{2,1,0:T(8,128)(2,1)}, u32[]{:S(2)}) copy-start(bf16[1,512,512]{2,1,0:T(8,128)(2,1)} %get-tuple-element.164) | copy-start | bytes 1572868 | tf_op jit(solution)/shard_map/while
  538.5 5.2 copy-start.2
  559.4 21.4 %copy-start.1 = (bf16[1,512,512]{2,1,0:T(8,128)(2,1)S(1)}, bf16[1,512,512]{2,1,0:T(8,128)(2,1)}, u32[]{:S(2)}) copy-start(bf16[1,512,512]{2,1,0:T(8,128)(2,1)} %get-tuple-element.164) | copy-start | bytes 1572868 | tf_op jit(solution)/shard_map/while
  615.7 21.4 %copy-start.1 = (bf16[1,512,512]{2,1,0:T(8,128)(2,1)S(1)}, bf16[1,512,512]{2,1,0:T(8,128)(2,1)}, u32[]{:S(2)}) copy-start(bf16[1,512,512]{2,1,0:T(8,128)(2,1)} %get-tuple-element.164) | copy-start | bytes 1572868 | tf_op jit(solution)/shard_map/while
  651.3 5.2 copy-start.2
  672.1 21.4 %copy-start.1 = (bf16[1,512,512]{2,1,0:T(8,128)(2,1)S(1)}, bf16[1,512,512]{2,1,0:T(8,128)(2,1)}, u32[]{:S(2)}) copy-start(bf16[1,512,512]{2,1,0:T(8,128)(2,1)} %get-tuple-element.164) | copy-start | bytes 1572868 | tf_op jit(solution)/shard_map/while
  707.7 5.2 copy-start.2
  728.5 21.4 %copy-start.1 = (bf16[1,512,512]{2,1,0:T(8,128)(2,1)S(1)}, bf16[1,512,512]{2,1,0:T(8,128)(2,1)}, u32[]{:S(2)}) copy-start(bf16[1,512,512]{2,1,0:T(8,128)(2,1)} %get-tuple-element.164) | copy-start | bytes 1572868 | tf_op jit(solution)/shard_map/while
  784.9 21.4 %copy-start.1 = (bf16[1,512,512]{2,1,0:T(8,128)(2,1)S(1)}, bf16[1,512,512]{2,1,0:T(8,128)(2,1)}, u32[]{:S(2)}) copy-start(bf16[1,512,512]{2,1,0:T(8,128)(2,1)} %get-tuple-element.164) | copy-start | bytes 1572868 | tf_op jit(solution)/shard_map/while
  820.4 5.2 copy-start.2
  841.3 21.4 %copy-start.1 = (bf16[1,512,512]{2,1,0:T(8,128)(2,1)S(1)}, bf16[1,512,512]{2,1,0:T(8,128)(2,1)}, u32[]{:S(2)}) copy-start(bf16[1,512,512]{2,1,0:T(8,128)(2,1)} %get-tuple-element.164) | copy-start | bytes 1572868 | tf_op jit(solution)/shard_map/while
  897.7 21.4 %copy-start.1 = (bf16[1,512,512]{2,1,0:T(8,128)(2,1)S(1)}, bf16[1,512,512]{2,1,0:T(8,128)(2,1)}, u32[]{:S(2)}) copy-start(bf16[1,512,512]{2,1,0:T(8,128)(2,1)} %get-tuple-element.164) | copy-start | bytes 1572868 | tf_op jit(solution)/shard_map/while
  933.2 5.2 copy-start.2
  953.7 34.7 %all-to-all-start.4 = ((f32[5120,1,1,128]{3,2,1,0:T(1,128)}), f32[5120,1,1,128]{3,2,1,0:T(1,128)}, u32[]{:S(2)}, u32[]{:S(2)}) async-start(f32[5120,1,1,128]{3,2,1,0:T(1,128)} %bitcast.123), calls=%async_computation.4 | async-start | bytes 5242880 | tf_op jit(solution)/shard_map/all_to_all | solution.py:92
  958.3 188.0 %all-gather.2.cloned.1.call-start = ((), (), s32[]{:S(2)}) async-start(), calls=%async_computation.5 | async-start | bytes 22282240 | tf_op jit(solution)/shard_map/all_gather | solution.py:108
  1001.7 7.6 copy-start.5
  1001.7 8.9 copy-start.4
  (7 other events, 35.7 us)
Sparse Core Ops, SparseCore 0:
  1008.7 137.5 all-gather.1
where the time goes:
time: 1260 us; the launch traced here: 1250 us
  local copies, waits for them, and re-layouts  705 us (56%)
  matrix products  216 us (17%)
  waiting for transfers between devices  171 us (14%)
  blocking collectives  119 us (9%)
  between operations  14.8 us (1%)
  other arithmetic  14.3 us (1%)
    gather x16, local copies, waits for them, and re-layouts, rows_of(): middle_rows = middle_core[middle_ids]  336 us
    all_gather x1, waiting for transfers between devices, body(): lax.all_gather(crossed_low, 'tables', axis=0, tiled=True)  135 us
    dot_general x16, matrix products, rows_of(): jnp.einsum('kdr,krm->kdm', first_rows, middle_rows, preferred_element_typ...  115 us
    dot_general x16, matrix products, rows_of(): jnp.einsum('kar,krd->kad', left_part, last_rows, preferred_element_type=j...  78.1 us
    reshape x16, local copies, waits for them, and re-layouts, rows_of(): left_part = left_part.reshape(item_count, D1 * D2, rank_size)  77.4 us
    reshape x16, local copies, waits for them, and re-layouts, pooled_block(): row_vecs = row_vecs.reshape(rows_here, BAG, D1 * D2 * D3)  73.3 us
    unnamed x1, blocking collectives  58.5 us
    gather x32, local copies, waits for them, and re-layouts, rows_of(): first_rows = first_core[first_ids].reshape(item_count, -1, rank_size)  49.3 us
  transfers between devices with their start and end apart: 3, of which 3 were waited for; matrix products, arithmetic and copies ran while one was open for 0% of the time, Pallas kernels for 0%

commit v1 on v0

v1 whole, which is shorter than its diff:
```python
import functools

import jax
import jax.numpy as jnp
from jax import lax
from jax.experimental import pallas as pl
from jax.experimental.pallas import tpu as pltpu
from jax.sharding import PartitionSpec as P

D1 = 8
D2 = 2
D3 = 8
BAG = 2
TILE = 32
LANES = 128

BF16 = jnp.bfloat16
F32 = jnp.float32
I32 = jnp.int32


def iota(shape, dim):
    return lax.broadcasted_iota(I32, shape, dim)


def dot(a, b):
    return jnp.dot(a, b, preferred_element_type=F32)


def dot_nt(a, b):
    return lax.dot_general(a, b, (((1,), (1,)), ((), ())), preferred_element_type=F32)


def order_kernel(groups, first_ref, middle_ref, dest_ref, owner_ref, slot_ref, rank_ref, sums_ref):
    blocks, width = first_ref.shape
    group_row = iota((groups, width), 0)
    before = (iota((width, width), 0) < iota((width, width), 1)).astype(BF16)

    def count(b, seen):
        hot = group_row == middle_ref[pl.ds(b, 1), :]
        ranks = dot(hot.astype(F32).astype(BF16), before)
        rank_ref[pl.ds(b, 1), :] = jnp.sum(jnp.where(hot, ranks + seen, 0.0), axis=0, keepdims=True)
        return seen + jnp.sum(hot.astype(F32), axis=1, keepdims=True)

    counts = lax.fori_loop(0, blocks, count, jnp.zeros((groups, 1), F32))
    tiles = jnp.floor((counts + (TILE - 1)) * (1.0 / TILE))
    tiles = jnp.broadcast_to(tiles, (groups, LANES))
    high = jnp.floor(tiles * (1.0 / 16))
    low = tiles - 16.0 * high
    above = (iota((groups, groups), 0) > iota((groups, groups), 1)).astype(BF16)
    offset = 16.0 * dot(above, high.astype(BF16)) + dot(above, low.astype(BF16))
    offset = offset[:, :1]
    tile_lane = iota((groups, owner_ref.shape[1]), 1)
    owner_ref[...] = jnp.sum((offset.astype(I32) <= tile_lane).astype(I32), axis=0, keepdims=True) - 1

    sums_ref[...] = jnp.zeros_like(sums_ref)
    lane_row = iota((LANES, width), 0)

    def place(b, carry):
        hot = group_row == middle_ref[pl.ds(b, 1), :]
        start = jnp.sum(jnp.where(hot, offset, 0.0), axis=0, keepdims=True) * TILE
        dest = (rank_ref[pl.ds(b, 1), :] + start).astype(I32)
        dest_ref[pl.ds(b, 1), :] = dest
        ids = first_ref[pl.ds(b, 1), :]
        at_lane = lane_row == (dest & (LANES - 1))
        high_id = jnp.where(at_lane, (ids >> 4).astype(F32), 0.0)
        low_id = jnp.where(at_lane, (ids & 15).astype(F32), 0.0)
        at_block = (lane_row == (dest >> 7)).astype(F32).astype(BF16)
        sums_ref[...] += dot_nt(jnp.concatenate([high_id, low_id], axis=0).astype(BF16), at_block)
        return carry

    lax.fori_loop(0, blocks, place, 0)
    slot_ref[...] = (16.0 * sums_ref[:LANES, :] + sums_ref[LANES:, :]).astype(I32)


def order(first_ids, middle_ids, groups):
    items = first_ids.size
    width = 256
    most_tiles = items // TILE + groups
    owners = -(-most_tiles // LANES) * LANES
    return pl.pallas_call(
        functools.partial(order_kernel, groups),
        out_shape=(
            jax.ShapeDtypeStruct((items // width, width), I32),
            jax.ShapeDtypeStruct((1, owners), I32),
            jax.ShapeDtypeStruct((LANES, LANES), I32),
        ),
        scratch_shapes=[
            pltpu.VMEM((items // width, width), F32),
            pltpu.VMEM((2 * LANES, LANES), F32),
        ],
        cost_estimate=pl.CostEstimate(flops=int(2e9), bytes_accessed=200000, transcendentals=0),
        name="order",
    )(first_ids.reshape(-1, width), middle_ids.reshape(-1, width))


def lookup_kernel(
    items,
    dest_ref,
    owner_ref,
    slot_ref,
    last_ids_ref,
    first_ref,
    middle_ref,
    last_ref,
    out_ref,
    pair_ref,
    last_by_d3_ref,
    left_ref,
    spread_ref,
    last_rows_ref,
    staged_ref,
    diag_ref,
):
    queries = items // BAG
    groups, rank, wide = middle_ref.shape
    rows, first_width = first_ref.shape

    def make_pair(g, carry):
        core = middle_ref[pl.ds(g, 1)].reshape(rank, wide)
        zero = jnp.zeros_like(core)
        pair_ref[pl.ds(g, 1), :rank, :wide] = core.reshape(1, rank, wide)
        pair_ref[pl.ds(g, 1), :rank, wide:] = zero.reshape(1, rank, wide)
        pair_ref[pl.ds(g, 1), rank:, :wide] = zero.reshape(1, rank, wide)
        pair_ref[pl.ds(g, 1), rank:, wide:] = core.reshape(1, rank, wide)
        return carry

    lax.fori_loop(0, groups, make_pair, 0)
    width = last_ref.shape[1]
    from_row, to_lane = iota((width, width), 0), iota((width, width), 1)
    swap = (to_lane == (from_row & (D3 - 1)) * rank + (from_row >> 3)).astype(F32).astype(BF16)
    last_by_d3_ref[...] = dot(last_ref[...], swap).astype(BF16)

    per_step = LANES // TILE
    steps = -(-(items // TILE + groups) // per_step)
    slot_lane = iota((LANES, LANES), 1)
    row_lane = iota((LANES, rows), 1)

    def make_left(step, carry):
        ids = jnp.sum(jnp.where(slot_lane == step, slot_ref[...], 0), axis=1, keepdims=True)
        hot = (row_lane == ids).astype(F32).astype(BF16)
        cores = dot(hot, first_ref[...]).astype(BF16)
        for t in range(per_step):
            owner = owner_ref[0, step * per_step + t]
            rows_t = cores[t * TILE : (t + 1) * TILE]
            stacked = jnp.concatenate(
                [rows_t[:, p * LANES : (p + 1) * LANES] for p in range(D1 // 2)], axis=0
            )
            pair = pair_ref[pl.ds(owner, 1)].reshape(2 * rank, 2 * wide)
            product = dot(stacked, pair)
            for p in range(D1 // 2):
                for half in range(2):
                    for s in range(TILE // 8):
                        spread_ref[t, pl.ds(s * 64 + 2 * p + half, 8, stride=D1), :] = product[
                            p * TILE + s * 8 : p * TILE + s * 8 + 8, half * wide : (half + 1) * wide
                        ]
            left_ref[pl.ds((step * per_step + t) * TILE, TILE)] = (
                spread_ref[t].reshape(TILE, D1, wide).astype(BF16)
            )
        return carry

    lax.fori_loop(0, steps, make_left, 0)

    group = TILE
    per_block = LANES // group
    blocks = queries // LANES
    id_lane = iota(last_ids_ref.shape, 1)
    low_half = iota((group, LANES), 1) < rank
    own = (iota((group, LANES), 1) >> 3) == (iota((group, LANES), 0) & 15)
    taps = D2 * D3 * LANES
    tap, spot = iota((taps, LANES), 0), iota((taps, LANES), 1)
    gather_own = (spot == (tap & (D1 - 1)) * (D2 * D3) + (tap >> 7)).astype(F32).astype(BF16)

    def make_block(block, carry):
        for k in range(BAG):
            ids = jnp.sum(
                jnp.where(id_lane == k * blocks + block, last_ids_ref[...], 0), axis=1, keepdims=True
            )
            hot = (row_lane == ids).astype(F32).astype(BF16)
            last_rows_ref[k] = dot(hot, last_by_d3_ref[...])

        def make_group(part, inner):
            base = block * LANES + part * group
            for k in range(BAG):
                for q in range(group):
                    at = dest_ref[k * queries + base + q]
                    staged_ref[k, pl.ds(q, 1)] = left_ref[pl.ds(at, 1)]
            right = jnp.concatenate(
                [staged_ref[k].reshape(group * D1, wide) for k in range(BAG)], axis=1
            )
            pieces = [[None] * BAG for _ in range(D2 * D3)]
            for k in range(BAG):
                for tile in range(D3 // 2):
                    both = last_rows_ref[k, pl.ds(part * group, group), tile * LANES : (tile + 1) * LANES]
                    low = jnp.where(low_half, both, 0.0)
                    high = jnp.where(low_half, 0.0, both)
                    pieces[2 * tile][k] = low
                    pieces[D3 + 2 * tile][k] = pltpu.roll(low, rank, 1)
                    pieces[2 * tile + 1][k] = pltpu.roll(high, rank, 1)
                    pieces[D3 + 2 * tile + 1][k] = high
            lasts = jnp.concatenate(
                [jnp.concatenate(p, axis=1) for p in pieces], axis=0
            ).astype(BF16)
            product = dot_nt(lasts, right)
            for e in range(D2 * D3):
                at = e * group
                mine = jnp.concatenate(
                    [product[at : at + 16, :LANES], product[at + 16 : at + 32, LANES:]], axis=0
                )
                diag_ref[pl.ds(part * group, group), e * LANES : (e + 1) * LANES] = jnp.where(
                    own, mine, 0.0
                ).astype(BF16)
            return inner

        lax.fori_loop(0, per_block, make_group, 0)
        out_ref[pl.ds(block * LANES, LANES), :] = dot(diag_ref[...], gather_own).astype(BF16)
        return carry

    lax.fori_loop(0, blocks, make_block, 0)


def lookup(dest, owner, slot, last_ids, core_first, core_middle, core_last):
    items = dest.size
    groups, rank, wide = core_middle.shape
    slots = -(-(items // TILE + groups) // (LANES // TILE)) * LANES
    smem = pl.BlockSpec(memory_space=pltpu.SMEM)
    vmem = pl.BlockSpec(memory_space=pltpu.VMEM)
    return pl.pallas_call(
        functools.partial(lookup_kernel, items),
        out_shape=jax.ShapeDtypeStruct((items // BAG, LANES), BF16),
        in_specs=[smem, smem, vmem, vmem, vmem, vmem, vmem],
        out_specs=vmem,
        scratch_shapes=[
            pltpu.VMEM((groups, 2 * rank, 2 * wide), BF16),
            pltpu.VMEM(core_last.shape, BF16),
            pltpu.VMEM((slots, D1, wide), BF16),
            pltpu.VMEM((LANES // TILE, TILE * D1, wide), F32),
            pltpu.VMEM((BAG, LANES, core_last.shape[1]), F32),
            pltpu.VMEM((BAG, TILE, D1, wide), BF16),
            pltpu.VMEM((LANES, D2 * D3 * LANES), BF16),
        ],
        compiler_params=pltpu.CompilerParams(vmem_limit_bytes=56 * 2**20),
        cost_estimate=pl.CostEstimate(flops=int(60e9), bytes_accessed=5000000, transcendentals=0),
        name="lookup",
    )(dest.reshape(-1), owner, slot, last_ids, core_first, core_middle, core_last)


def top_kernel(
    core_ref, recv_ref, own_ref, other_ref, down_ref, up_ref, bias_ref, top_bias_ref, out_weight_ref,
    logit_ref, first_half_ref, second_half_ref, sum_ref,
):
    step = pl.program_id(0)
    depth = own_ref.shape[1]

    @pl.when(step == 0)
    def _():
        first = jnp.concatenate(
            [recv_ref[t] for t in range(recv_ref.shape[0])], axis=1
        ).astype(F32)
        crossed = first
        for layer in range(down_ref.shape[0]):
            low = dot(crossed.astype(BF16), down_ref[layer]).astype(BF16)
            lifted = dot(low, up_ref[layer])
            crossed = first * (lifted + bias_ref[layer : layer + 1, :].astype(F32)) + crossed
        crossed = crossed.astype(BF16)
        swap = core_ref[0] == 1

        @pl.when(swap)
        def _():
            first_half_ref[...] = crossed[:, depth:]
            second_half_ref[...] = crossed[:, :depth]

        @pl.when(jnp.logical_not(swap))
        def _():
            first_half_ref[...] = crossed[:, :depth]
            second_half_ref[...] = crossed[:, depth:]

        sum_ref[...] = jnp.zeros_like(sum_ref)

    hidden = dot(first_half_ref[...], own_ref[0]) + dot(second_half_ref[...], other_ref[0])
    hidden = jnp.maximum(hidden + top_bias_ref[0].astype(F32), 0.0).astype(BF16).astype(F32)
    sum_ref[...] += hidden * out_weight_ref[0].astype(F32)

    @pl.when(step == pl.num_programs(0) - 1)
    def _():
        logit_ref[...] = jnp.sum(sum_ref[...], axis=1, keepdims=True)


def top(core, received, own, other, cross_down, cross_up, cross_bias, top_bias, out_weight):
    shards, depth, hid = own.shape
    queries = received.shape[1]

    def whole(shape):
        return pl.BlockSpec(shape, lambda t: (0,) * len(shape))

    return pl.pallas_call(
        top_kernel,
        grid=(shards,),
        out_shape=jax.ShapeDtypeStruct((queries, 1), F32),
        in_specs=[
            pl.BlockSpec(memory_space=pltpu.SMEM),
            whole(received.shape),
            pl.BlockSpec((1, depth, hid), lambda t: (t, 0, 0)),
            pl.BlockSpec((1, depth, hid), lambda t: (t, 0, 0)),
            whole(cross_down.shape),
            whole(cross_up.shape),
            whole(cross_bias.shape),
            pl.BlockSpec((1, 1, hid), lambda t: (t, 0, 0)),
            pl.BlockSpec((1, 1, hid), lambda t: (t, 0, 0)),
        ],
        out_specs=whole((queries, 1)),
        scratch_shapes=[
            pltpu.VMEM((queries, depth), BF16),
            pltpu.VMEM((queries, depth), BF16),
            pltpu.VMEM((queries, hid), F32),
        ],
        compiler_params=pltpu.CompilerParams(vmem_limit_bytes=56 * 2**20),
        cost_estimate=pl.CostEstimate(flops=int(8e9), bytes_accessed=24000000, transcendentals=0),
        name="top",
    )(
        core, received, own, other, cross_down, cross_up, cross_bias,
        top_bias.reshape(shards, 1, hid), out_weight.reshape(shards, 1, hid),
    )


def body(
    core_first,
    core_middle,
    core_last,
    idx_first,
    idx_middle,
    idx_last,
    bag_lengths,
    cross_down,
    cross_up,
    cross_bias,
    top_weight,
    top_bias,
    out_weight,
    prior,
):
    shards = lax.axis_size("tables")
    replicas = lax.axis_size("replica")
    queries = idx_first.shape[2]

    core = lax.rem(lax.axis_index("replica"), 2)
    depth = top_weight.shape[0] // 2
    part = lax.dynamic_slice_in_dim(top_weight, core * depth, depth, axis=0)
    own = lax.all_gather(part, "tables", axis=0)
    other = lax.ppermute(own, "replica", [(i, i ^ 1) for i in range(replicas)])

    in_bag = jnp.arange(BAG, dtype=I32)[None, :, None] < bag_lengths[0, 0].T[:, None, :]

    def by_table(values):
        return jnp.transpose(values[0, 0], (1, 2, 0))

    sent = jnp.concatenate(
        [
            by_table(idx_first),
            by_table(idx_middle),
            jnp.where(in_bag, by_table(idx_last), -1),
        ],
        axis=1,
    )
    at_owner = lax.all_to_all(sent, "tables", split_axis=0, concat_axis=0, tiled=True)
    at_owner = jnp.transpose(at_owner, (1, 0, 2))
    first_ids, middle_ids, last_ids = (
        at_owner[BAG * i : BAG * (i + 1)].reshape(-1, LANES) for i in range(3)
    )
    dest, owner, slot = order(first_ids, middle_ids, core_middle.shape[1])
    pooled = lookup(
        dest, owner, slot, last_ids.T, core_first[0], core_middle[0], core_last[0]
    )
    received = lax.all_to_all(
        pooled.reshape(shards, queries, LANES), "tables", split_axis=0, concat_axis=0, tiled=True
    )
    summed = top(
        core.reshape(1), received, own, other, cross_down, cross_up, cross_bias, top_bias, out_weight
    )
    logits = summed[:, 0] + prior[0, 0]
    clicks = jax.nn.sigmoid(logits)
    request_sum = lax.psum(jnp.sum(clicks), "replica")
    click_share = replicas * queries * clicks / request_sum
    return (logits[None, None], click_share[None, None])


def solution(mesh):
    in_specs = (
        P("tables", None, None),
        P("tables", None, None, None),
        P("tables", None, None),
        P("replica", "tables", None, None, None),
        P("replica", "tables", None, None, None),
        P("replica", "tables", None, None, None),
        P("replica", "tables", None, None),
        P(),
        P(),
        P(),
        P(None, "tables"),
        P(),
        P(),
        P("replica", "tables", None),
    )
    out_specs = (P("replica", "tables", None), P("replica", "tables", None))
    return jax.shard_map(body, mesh=mesh, in_specs=in_specs, out_specs=out_specs, check_vma=False)
```

time: 1260 us -> 321 us (0.25)
  local copies, waits for them, and re-layouts: 705 us -> 8.04 us
  matrix products: 216 us -> 0 us
  Pallas kernels: 0 us -> 169 us
  blocking collectives: 119 us -> 28.3 us
  waiting for transfers between devices: 171 us -> 92 us
    gather x80 -> x0, local copies, waits for them, and re-layouts: 435 us -> none  [the longest x16 336 us: rows_of(): middle_rows = middle_core[middle_ids]]
    dot_general x35 -> x0, matrix products: 216 us -> none  [the longest x16 115 us: rows_of(): jnp.einsum('kdr,krm->kdm', first_rows, middle_rows, preferred_element_typ...]
    reshape x64 -> x4, local copies, waits for them, and re-layouts: 204 us -> 2.03 us  [the longest x2 0.82 us: body(): at_owner[BAG * i:BAG * (i + 1)].reshape(-1, LANES)]
    pallas_call x0 -> x3, Pallas kernels: none -> 169 us  [the longest x1 128 us: lookup(): pl.pallas_call(functools.partial(lookup_kernel, items), out_shape=jax.Sha...]
    all_gather x1, waiting for transfers between devices: 135 us -> 74.7 us  [body(): own = lax.all_gather(part, 'tables', axis=0)]
    unnamed x1 -> x0, blocking collectives: 58.5 us -> none
    convert_element_type x17 -> x0, local copies, waits for them, and re-layouts: 32.7 us -> none  [the longest x16 31.8 us: rows_of(): left_part = jnp.einsum('kdr,krm->kdm', first_rows, middle_rows, preferred...]
    all_to_all x3 -> x1, blocking collectives: 33.6 us -> 12.6 us  [body(): lax.all_to_all(sent, 'tables', split_axis=0, concat_axis=0, tiled=True)]
  transfers between devices with their start and end apart: 3 -> 3, of which waited for: 3 -> 2; matrix products, arithmetic and copies ran while one was open for 0% -> 2% of each run, Pallas kernels for 0% -> 46%
where the time goes in v1:
time: 321 us; the launch traced here: 320 us
  Pallas kernels  169 us (53%)
  waiting for transfers between devices  92 us (29%)
  blocking collectives  28.3 us (9%)
  between operations  14.1 us (4%)
  local copies, waits for them, and re-layouts  8.04 us (3%)
  other arithmetic  4.64 us (1%)
  starting transfers between devices  4.56 us (1%)
    pallas_call x1, Pallas kernels, lookup(): pl.pallas_call(functools.partial(lookup_kernel, items), out_shape=jax.Sha...  128 us
    all_gather x1, waiting for transfers between devices, body(): own = lax.all_gather(part, 'tables', axis=0)  74.7 us
    pallas_call x1, Pallas kernels, order(): pl.pallas_call(functools.partial(order_kernel, groups), out_shape=(jax.Sh...  20.2 us
    pallas_call x1, Pallas kernels, top(): pl.pallas_call(top_kernel, grid=(shards,), out_shape=jax.ShapeDtypeStruct...  20.2 us
    all_to_all x1, waiting for transfers between devices, body(): lax.all_to_all(pooled.reshape(shards, queries, LANES), 'tables', split_ax...  17.3 us
    psum x1, blocking collectives, body(): request_sum = lax.psum(jnp.sum(clicks), 'replica')  15.8 us
    all_to_all x1, blocking collectives, body(): lax.all_to_all(sent, 'tables', split_axis=0, concat_axis=0, tiled=True)  12.6 us
  transfers between devices with their start and end apart: 3, of which 2 were waited for; matrix products, arithmetic and copies ran while one was open for 2% of the time, Pallas kernels for 46%

profile of v1, /device:TPU:1, one launch (start us, length us, event | category | flops | bytes accessed | tf_op | source)
XLA Modules:
  0.0 320.2 jit_solution(5766015960400994374)
XLA Ops:
  7.2 0.0 copy-start
  7.2 0.0 all-gather.3.cloned.1.call-start
  7.2 1.2 copy-done
  8.4 0.9 constant_dynamic-slice_fusion
  9.3 0.0 all-gather.3.cloned.1.call-update
  9.3 74.7 %all-gather.3.cloned.1.call-done = bf16[16384,256]{1,0:T(8,128)(2,1)} async-done(((bf16[1024,256]{1,0:T(8,128)(2,1)}), bf16[16384,256]{1,0:T(8,128)(2,1)}) %all-gather.3.cloned.1.call-update) | async-done | bytes 8388624 | tf_op jit(solution)/shard_map/all_gather | solution.py:349
  84.0 0.7 collective-permute-start
  84.7 0.8 compare_select_fusion
  85.5 0.9 pad_add_fusion
  86.4 12.6 %all_to_all.10 = s32[16,6,320]{2,1,0:T(8,128)S(1)} all-to-all(s32[16,6,320]{2,1,0:T(8,128)S(1)} %pad_add_fusion), channel_id=1, replica_groups=mesh['tables'=16,'replica'=8] {'tables'}, dimensions={0} | all-to-all | bytes 245760 | tf_op jit(solution)/shard_map/all_to_all | solution.py:365
  99.0 0.1 fusion.1
  99.1 0.7 reshape_reshape.6.first_ref
  99.8 0.7 reshape_reshape.7.middle_ref
  100.5 20.2 %order.1 = (s32[40,256]{1,0:T(8,128)}, s32[1,512]{1,0:T(1,128)}, s32[128,128]{1,0:T(8,128)}) custom-call(s32[40,256]{1,0:T(8,128)} %reshape_reshape.6.first_ref, s32[40,256]{1,0:T(8,128)} %reshape_reshape.7.middle_ref), custom_call_target="tpu_custom_call" | custom-call | flops 2000000000 | bytes 200000 | tf_op jit(solution)/shard_map/order/pallas_call | solution.py:81
  120.7 1.4 copy.24
  122.1 0.1 reshape.27
  122.2 0.7 copy.21
  122.9 128.2 %lookup.1 = bf16[5120,128]{1,0:T(8,128)(2,1)} custom-call(s32[10240]{0:T(1024)} %bitcast.28, s32[1,512]{1,0:T(1,128)} %get-tuple-element.6.owner_ref, s32[128,128]{1,0:T(8,128)} %get-tuple-element.7.slot_ref, s32[128,80]{1,0:T(8,128)} %bitcast.25, bf16[512,512]{1,0:T(8,128)(2,1)} %bitcast.34, bf16[80,64,128]{2,1,0:T(8,128)(2,1)} %bitcast.33, ...), custom_call_target="tpu_custom_call" | custom-call | flops 60000002048 | bytes 5000000 | tf_op jit(solution)/shard_map/lookup/pallas_call | solution.py:228
  251.1 3.8 %all-to-all-start.1 = ((bf16[16,320,128]{2,1,0:T(8,128)(2,1)}), bf16[16,320,128]{2,1,0:T(8,128)(2,1)S(1)}, u32[]{:S(2)}, u32[]{:S(2)}) async-start(bf16[16,320,128]{2,1,0:T(8,128)(2,1)} %bitcast.23), calls=%async_computation.1 | async-start | bytes 2621440 | tf_op jit(solution)/shard_map/all_to_all | solution.py:374
  255.0 0.0 copy-done.2
  255.0 0.6 reshape.32.top_bias_ref
  255.6 0.0 copy-done.3
  255.6 0.6 reshape.33.out_weight_ref
  256.2 0.0 copy-done.4
  256.2 17.3 %all-to-all-done.1.recv_ref = bf16[16,320,128]{2,1,0:T(8,128)(2,1)S(1)} async-done(((bf16[16,320,128]{2,1,0:T(8,128)(2,1)}), bf16[16,320,128]{2,1,0:T(8,128)(2,1)S(1)}, u32[]{:S(2)}, u32[]{:S(2)}) %all-to-all-start.1) | async-done | bytes 1310752 | tf_op jit(solution)/shard_map/all_to_all | solution.py:374
  273.5 0.0 collective-permute-done.other_ref
  273.5 1.1 copy-done.1
  274.6 20.2 %top.1 = f32[320,1]{1,0:T(8,128)} custom-call(s32[1]{0:T(128)} %bitcast.core_ref, bf16[16,320,128]{2,1,0:T(8,128)(2,1)} %copy-done.1, bf16[16,1024,256]{2,1,0:T(8,128)(2,1)} %bitcast.32, bf16[16,1024,256]{2,1,0:T(8,128)(2,1)} %collective-permute-done.other_ref, bf16[2,2048,256]{2,1,0:T(8,128)(2,1)} %down_ref.1, bf16[2,256,2048]{2,1,0:T(8,128)(2,1)} %up_ref.1, ...), custom_call_target="tpu_custom_call" | custom-call | flops 8000000000 | bytes 24000000 | tf_op jit(solution)/shard_map/top/pallas_call | solution.py:296
  294.7 1.1 reduce
  295.8 0.6 fusion
  296.4 15.8 %psum.7 = f32[]{:T(128)} all-reduce(f32[]{:T(128)} %fusion), channel_id=1, replica_groups=mesh['tables'=16,'replica'=8] {'replica'}, use_global_device_ids=true, to_apply=%region_1.2 | all-reduce | flops 1 | bytes 8 | tf_op jit(solution)/shard_map/psum | solution.py:382
  312.2 1.2 multiply_divide_fusion
  (8 shorter events, 0.0 us)
Async XLA Ops:
  7.2 1.2 copy-start
  7.2 76.8 %all-gather.3.cloned.1.call-start = ((), (), s32[]{:S(2)}) async-start(), calls=%async_computation.2 | async-start | bytes 8912896 | tf_op jit(solution)/shard_map/all_gather | solution.py:349
  84.0 189.5 %collective-permute-start = (bf16[16,1024,256]{2,1,0:T(8,128)(2,1)}, bf16[16,1024,256]{2,1,0:T(8,128)(2,1)}, u32[]{:S(2)}, u32[]{:S(2)}) collective-permute-start(bf16[16,1024,256]{2,1,0:T(8,128)(2,1)} %bitcast.31), channel_id=1, source_target_pairs={{0,1},{1,0},{2,3},{3,2},{4,5},{5,4},{6,7},{7,6},{8,9},{9,8},{10,11... | collective-permute-start | bytes 25165832 | tf_op jit(solution)/shard_map/ppermute | solution.py:350
  251.1 3.9 %copy-start.2 = (bf16[4096]{0:T(1024)(128)(2,1)S(1)}, bf16[4096]{0:T(1024)(128)(2,1)}, u32[]{:S(2)}) copy-start(bf16[4096]{0:T(1024)(128)(2,1)} %param.25) | copy-start | bytes 24580
  251.1 4.5 %copy-start.3 = (bf16[4096]{0:T(1024)(128)(2,1)S(1)}, bf16[4096]{0:T(1024)(128)(2,1)}, u32[]{:S(2)}) copy-start(bf16[4096]{0:T(1024)(128)(2,1)} %param.26) | copy-start | bytes 24580
  251.1 5.1 %copy-start.4 = (f32[1,1,320]{2,1,0:T(1,128)S(1)}, f32[1,1,320]{2,1,0:T(1,128)}, u32[]{:S(2)}) copy-start(f32[1,1,320]{2,1,0:T(1,128)} %param.27) | copy-start | bytes 3844
  251.1 22.4 %all-to-all-start.1 = ((bf16[16,320,128]{2,1,0:T(8,128)(2,1)}), bf16[16,320,128]{2,1,0:T(8,128)(2,1)S(1)}, u32[]{:S(2)}, u32[]{:S(2)}) async-start(bf16[16,320,128]{2,1,0:T(8,128)(2,1)} %bitcast.23), calls=%async_computation.1 | async-start | bytes 2621440 | tf_op jit(solution)/shard_map/all_to_all | solution.py:374
  273.5 1.1 copy-start.1
Sparse Core Ops, SparseCore 0:
  10.2 73.8 all-gather.2

commit v2 on v1

v2 whole, which is shorter than its diff:
```python
import functools

import jax
import jax.numpy as jnp
from jax import lax
from jax.experimental import pallas as pl
from jax.experimental.pallas import tpu as pltpu
from jax.sharding import PartitionSpec as P

D1 = 8
D2 = 2
D3 = 8
BAG = 2
TILE = 32
LANES = 128
STEP = 512

BF16 = jnp.bfloat16
F32 = jnp.float32
I32 = jnp.int32
MESH = pl.DeviceIdType.MESH


def iota(shape, dim):
    return lax.broadcasted_iota(I32, shape, dim)


def dot(a, b):
    return jnp.dot(a, b, preferred_element_type=F32)


def dot_nt(a, b):
    return lax.dot_general(a, b, (((1,), (1,)), ((), ())), preferred_element_type=F32)


def order_kernel(groups, first_ref, middle_ref, dest_ref, owner_ref, slot_ref, rank_ref, sums_ref):
    blocks, width = first_ref.shape
    group_row = iota((groups, width), 0)
    before = (iota((width, width), 0) < iota((width, width), 1)).astype(BF16)
    together = 8

    def hot_rows(first):
        ids = middle_ref[pl.ds(first, together), :]
        return [group_row == ids[u : u + 1, :] for u in range(together)]

    def count(step, seen):
        hots = hot_rows(step * together)
        ones = jnp.concatenate([h.astype(F32) for h in hots], axis=0)
        ranks = dot(ones.astype(BF16), before)
        sizes = jnp.sum(ones, axis=1, keepdims=True)
        rows = []
        for u in range(together):
            at = slice(u * groups, (u + 1) * groups)
            rows.append(jnp.sum(jnp.where(hots[u], ranks[at] + seen, 0.0), axis=0, keepdims=True))
            seen = seen + sizes[at]
        rank_ref[pl.ds(step * together, together), :] = jnp.concatenate(rows, axis=0)
        return seen

    counts = lax.fori_loop(0, blocks // together, count, jnp.zeros((groups, 1), F32))
    tiles = jnp.floor((counts + (TILE - 1)) * (1.0 / TILE))
    tiles = jnp.broadcast_to(tiles, (groups, LANES))
    high = jnp.floor(tiles * (1.0 / 16))
    low = tiles - 16.0 * high
    above = (iota((groups, groups), 0) > iota((groups, groups), 1)).astype(BF16)
    offset = 16.0 * dot(above, high.astype(BF16)) + dot(above, low.astype(BF16))
    offset = offset[:, :1]
    tile_lane = iota((groups, owner_ref.shape[1]), 1)
    owner_ref[...] = jnp.sum((offset.astype(I32) <= tile_lane).astype(I32), axis=0, keepdims=True) - 1

    sums_ref[...] = jnp.zeros_like(sums_ref)
    lane_row = iota((LANES, width), 0)

    def place(step, carry):
        first = step * together
        hots = hot_rows(first)
        starts = [jnp.sum(jnp.where(h, offset, 0.0), axis=0, keepdims=True) for h in hots]
        dests = (rank_ref[pl.ds(first, together), :] + TILE * jnp.concatenate(starts, axis=0)).astype(I32)
        dest_ref[pl.ds(first, together), :] = dests
        ids = first_ref[pl.ds(first, together), :]
        lanes, highs, lows, rows = dests & (LANES - 1), (ids >> 4).astype(F32), (ids & 15).astype(F32), dests >> 7
        values, spots = [], []
        for u in range(together):
            at = slice(u, u + 1)
            at_lane = lane_row == lanes[at]
            values.append(
                jnp.concatenate(
                    [jnp.where(at_lane, highs[at], 0.0), jnp.where(at_lane, lows[at], 0.0)], axis=0
                ).astype(BF16)
            )
            spots.append((lane_row == rows[at]).astype(F32).astype(BF16))
        sums_ref[...] += dot_nt(jnp.concatenate(values, axis=1), jnp.concatenate(spots, axis=1))
        return carry

    lax.fori_loop(0, blocks // together, place, 0)
    slot_ref[...] = (16.0 * sums_ref[:LANES, :] + sums_ref[LANES:, :]).astype(I32)


def order(first_ids, middle_ids, groups):
    items = first_ids.size
    width = 256
    most_tiles = items // TILE + groups
    owners = -(-most_tiles // LANES) * LANES
    return pl.pallas_call(
        functools.partial(order_kernel, groups),
        out_shape=(
            jax.ShapeDtypeStruct((items // width, width), I32),
            jax.ShapeDtypeStruct((1, owners), I32),
            jax.ShapeDtypeStruct((LANES, LANES), I32),
        ),
        scratch_shapes=[
            pltpu.VMEM((items // width, width), F32),
            pltpu.VMEM((2 * LANES, LANES), F32),
        ],
        cost_estimate=pl.CostEstimate(flops=int(2e9), bytes_accessed=200000, transcendentals=0),
        name="order",
    )(first_ids.reshape(-1, width), middle_ids.reshape(-1, width))


def lookup_kernel(
    items,
    dest_ref,
    owner_ref,
    slot_ref,
    last_ids_ref,
    first_ref,
    middle_ref,
    last_ref,
    out_ref,
    pair_ref,
    last_by_d3_ref,
    left_ref,
    spread_ref,
    cores_a_ref,
    cores_b_ref,
    last_a_ref,
    last_b_ref,
    staged_ref,
    diag_a_ref,
    diag_b_ref,
    gather_own_ref,
):
    queries = items // BAG
    groups, rank, wide = middle_ref.shape
    rows, first_width = first_ref.shape

    def make_pair(g, carry):
        core = middle_ref[pl.ds(g, 1)].reshape(rank, wide)
        zero = jnp.zeros_like(core)
        pair_ref[pl.ds(g, 1), :rank, :wide] = core.reshape(1, rank, wide)
        pair_ref[pl.ds(g, 1), :rank, wide:] = zero.reshape(1, rank, wide)
        pair_ref[pl.ds(g, 1), rank:, :wide] = zero.reshape(1, rank, wide)
        pair_ref[pl.ds(g, 1), rank:, wide:] = core.reshape(1, rank, wide)
        return carry

    lax.fori_loop(0, groups, make_pair, 0)
    width = last_ref.shape[1]
    from_row, to_lane = iota((width, width), 0), iota((width, width), 1)
    swap = (to_lane == (from_row & (D3 - 1)) * rank + (from_row >> 3)).astype(F32).astype(BF16)
    last_by_d3_ref[...] = dot(last_ref[...], swap).astype(BF16)

    per_step = STEP // TILE
    pairs = left_ref.shape[0] // (2 * STEP)
    slot_lane = iota((LANES, LANES), 1)
    row_lane = iota((LANES, rows), 1)

    def hot_of(ids):
        return (row_lane == ids).astype(F32).astype(BF16)

    def gather_first(step, to_ref):
        hots = []
        for c in range(STEP // LANES):
            column = step * (STEP // LANES) + c
            hots.append(
                hot_of(jnp.sum(jnp.where(slot_lane == column, slot_ref[...], 0), axis=1, keepdims=True))
            )
        to_ref[...] = dot(jnp.concatenate(hots, axis=0), first_ref[...]).astype(BF16)

    def make_left(step, from_ref):
        for t in range(per_step):
            owner = owner_ref[0, step * per_step + t]
            stacked = jnp.concatenate(
                [
                    from_ref[t * TILE : (t + 1) * TILE, p * LANES : (p + 1) * LANES]
                    for p in range(D1 // 2)
                ],
                axis=0,
            )
            pair = pair_ref[pl.ds(owner, 1)].reshape(2 * rank, 2 * wide)
            product = dot(stacked, pair)
            for p in range(D1 // 2):
                for half in range(2):
                    for s in range(TILE // 8):
                        spread_ref[t, pl.ds(s * 64 + 2 * p + half, 8, stride=D1), :] = product[
                            p * TILE + s * 8 : p * TILE + s * 8 + 8, half * wide : (half + 1) * wide
                        ]
            left_ref[pl.ds((step * per_step + t) * TILE, TILE)] = (
                spread_ref[t].reshape(TILE, D1, wide).astype(BF16)
            )

    gather_first(0, cores_a_ref)

    def left_pair(pair, carry):
        gather_first(2 * pair + 1, cores_b_ref)
        make_left(2 * pair, cores_a_ref)
        gather_first(2 * pair + 2, cores_a_ref)
        make_left(2 * pair + 1, cores_b_ref)
        return carry

    lax.fori_loop(0, pairs, left_pair, 0)

    group = TILE
    per_block = LANES // group
    blocks = queries // LANES
    id_lane = iota(last_ids_ref.shape, 1)
    low_half = iota((group, LANES), 1) < rank
    own = (iota((group, LANES), 1) >> 3) == (iota((group, LANES), 0) & 15)
    taps = D2 * D3 * LANES
    tap, spot = iota((taps, LANES), 0), iota((taps, LANES), 1)
    gather_own_ref[...] = (spot == (tap & (D1 - 1)) * (D2 * D3) + (tap >> 7)).astype(F32).astype(BF16)

    def gather_last(block, to_ref):
        hots = [
            hot_of(
                jnp.sum(
                    jnp.where(id_lane == k * blocks + block, last_ids_ref[...], 0), axis=1, keepdims=True
                )
            )
            for k in range(BAG)
        ]
        to_ref[...] = dot(jnp.concatenate(hots, axis=0), last_by_d3_ref[...])

    def make_group(block, part, which, from_ref, diag_ref):
        base = block * LANES + part * group
        for k in range(BAG):
            for q in range(group):
                at = dest_ref[k * queries + base + q]
                staged_ref[which, k, q] = left_ref[at]
        right = jnp.concatenate(
            [staged_ref[which, k].reshape(group * D1, wide) for k in range(BAG)], axis=1
        )
        pieces = [[None] * BAG for _ in range(D2 * D3)]
        for k in range(BAG):
            start = k * LANES + part * group
            for tile in range(D3 // 2):
                both = from_ref[start : start + group, tile * LANES : (tile + 1) * LANES]
                low = jnp.where(low_half, both, 0.0)
                high = jnp.where(low_half, 0.0, both)
                pieces[2 * tile][k] = low
                pieces[D3 + 2 * tile][k] = pltpu.roll(low, rank, 1)
                pieces[2 * tile + 1][k] = pltpu.roll(high, rank, 1)
                pieces[D3 + 2 * tile + 1][k] = high
        lasts = jnp.concatenate([jnp.concatenate(p, axis=1) for p in pieces], axis=0).astype(BF16)
        product = dot_nt(lasts, right)
        for e in range(D2 * D3):
            at = e * group
            mine = jnp.concatenate(
                [product[at : at + 16, :LANES], product[at + 16 : at + 32, LANES:]], axis=0
            )
            diag_ref[part * group : (part + 1) * group, e * LANES : (e + 1) * LANES] = jnp.where(
                own, mine, 0.0
            ).astype(BF16)

    def make_block(block, which, from_ref, diag_ref):
        for part in range(per_block):
            make_group(block, part, which + part, from_ref, diag_ref)
        out_ref[pl.ds(block * LANES, LANES), :] = dot(diag_ref[...], gather_own_ref[...]).astype(BF16)

    gather_last(0, last_a_ref)

    def block_pair(pair, carry):
        gather_last(2 * pair + 1, last_b_ref)
        make_block(2 * pair, 0, last_a_ref, diag_a_ref)
        gather_last(jnp.minimum(2 * pair + 2, blocks - 1), last_a_ref)
        make_block(2 * pair + 1, per_block, last_b_ref, diag_b_ref)
        return carry

    lax.fori_loop(0, blocks // 2, block_pair, 0)


def lookup(dest, owner, slot, last_ids, core_first, core_middle, core_last):
    items = dest.size
    groups, rank, wide = core_middle.shape
    slots = -(-(items + groups * TILE) // (2 * STEP)) * 2 * STEP
    smem = pl.BlockSpec(memory_space=pltpu.SMEM)
    vmem = pl.BlockSpec(memory_space=pltpu.VMEM)
    return pl.pallas_call(
        functools.partial(lookup_kernel, items),
        out_shape=jax.ShapeDtypeStruct((items // BAG, LANES), BF16),
        in_specs=[smem, smem, vmem, vmem, vmem, vmem, vmem],
        out_specs=vmem,
        scratch_shapes=[
            pltpu.VMEM((groups, 2 * rank, 2 * wide), BF16),
            pltpu.VMEM(core_last.shape, BF16),
            pltpu.VMEM((slots, D1, wide), BF16),
            pltpu.VMEM((STEP // TILE, TILE * D1, wide), F32),
            pltpu.VMEM((STEP, core_first.shape[1]), BF16),
            pltpu.VMEM((STEP, core_first.shape[1]), BF16),
            pltpu.VMEM((BAG * LANES, core_last.shape[1]), F32),
            pltpu.VMEM((BAG * LANES, core_last.shape[1]), F32),
            pltpu.VMEM((2 * LANES // TILE, BAG, TILE, D1, wide), BF16),
            pltpu.VMEM((LANES, D2 * D3 * LANES), BF16),
            pltpu.VMEM((LANES, D2 * D3 * LANES), BF16),
            pltpu.VMEM((D2 * D3 * LANES, LANES), BF16),
        ],
        compiler_params=pltpu.CompilerParams(vmem_limit_bytes=56 * 2**20),
        cost_estimate=pl.CostEstimate(flops=int(60e9), bytes_accessed=5000000, transcendentals=0),
        name="lookup",
    )(dest.reshape(-1), owner, slot, last_ids, core_first, core_middle, core_last)


def tail_kernel(
    pooled_ref, weight_ref, down_ref, up_ref, bias_ref, top_bias_ref, out_weight_ref, prior_ref,
    logit_ref, share_ref,
    recv_ref, mine_ref, theirs_ref, wide_ref, down_v, up_v, part_ref, part_in_ref, click_ref, sum_ref,
    pooled_send, pooled_recv, local_sem, weight_sem, pair_send, pair_recv, part_send, part_recv,
    click_send, click_recv,
):
    shards, queries, lanes = pooled_ref.shape
    replicas = lax.axis_size("replica")
    me, rep = lax.axis_index("tables"), lax.axis_index("replica")
    sibling = rep + 1 - 2 * lax.rem(rep, 2)

    fetches = [
        pltpu.make_async_copy(down_ref, down_v, weight_sem.at[0]),
        pltpu.make_async_copy(up_ref, up_v, weight_sem.at[1]),
        pltpu.make_async_copy(weight_ref, wide_ref, weight_sem.at[2]),
    ]
    for fetch in fetches:
        fetch.start()
    keep = pltpu.make_async_copy(pooled_ref.at[me], recv_ref.at[me], local_sem)
    keep.start()

    barrier = pltpu.get_barrier_semaphore()
    for i in range(1, shards):
        pl.semaphore_signal(
            barrier, inc=1, device_id={"tables": lax.rem(me + i, shards)}, device_id_type=MESH
        )
    for i in range(1, replicas):
        pl.semaphore_signal(
            barrier, inc=1, device_id={"replica": lax.rem(rep + i, replicas)}, device_id_type=MESH
        )
    pl.semaphore_wait(barrier, shards + replicas - 2)

    sends = []
    for i in range(1, shards):
        to = lax.rem(me + i, shards)
        sends.append(
            pltpu.make_async_remote_copy(
                src_ref=pooled_ref.at[to],
                dst_ref=recv_ref.at[me],
                send_sem=pooled_send.at[i],
                recv_sem=pooled_recv.at[i],
                device_id={"tables": to},
                device_id_type=MESH,
            )
        )
    for send in sends:
        send.start()
    keep.wait()
    for send in sends:
        send.wait()
    fetches[0].wait()
    fetches[1].wait()

    first = jnp.concatenate([recv_ref[t] for t in range(shards)], axis=1).astype(F32)
    crossed = first
    for layer in range(down_v.shape[0]):
        low = dot(crossed.astype(BF16), down_v[layer]).astype(BF16)
        lifted = dot(low, up_v[layer])
        crossed = first * (lifted + bias_ref[layer : layer + 1, :].astype(F32)) + crossed
    mine_ref[...] = crossed.astype(BF16)
    pair = pltpu.make_async_remote_copy(
        src_ref=mine_ref, dst_ref=theirs_ref, send_sem=pair_send, recv_sem=pair_recv,
        device_id={"replica": sibling}, device_id_type=MESH,
    )
    pair.start()
    fetches[2].wait()

    def summed(rows_ref):
        sum_ref[...] = jnp.zeros_like(sum_ref)

        def step(t, carry):
            weight = jnp.concatenate([wide_ref[2 * t], wide_ref[2 * t + 1]], axis=1)
            hidden = dot(rows_ref[...], weight)
            for half in range(2):
                at = 2 * t + half
                unit = hidden[:, half * lanes : (half + 1) * lanes] + top_bias_ref[pl.ds(at, 1), :]
                unit = jnp.maximum(unit, 0.0).astype(BF16).astype(F32)
                sum_ref[:queries] += unit * out_weight_ref[pl.ds(at, 1), :]
            return carry

        lax.fori_loop(0, shards // 2, step, 0)
        return jnp.sum(jnp.transpose(sum_ref[...]), axis=0, keepdims=True)

    ours = summed(mine_ref)
    pair.wait()
    part_ref[...] = jnp.broadcast_to(summed(theirs_ref), part_ref.shape)
    back = pltpu.make_async_remote_copy(
        src_ref=part_ref, dst_ref=part_in_ref, send_sem=part_send, recv_sem=part_recv,
        device_id={"replica": sibling}, device_id_type=MESH,
    )
    back.start()
    back.wait()
    logits = (ours + part_in_ref[:1])[:, :queries] + prior_ref[...]
    logit_ref[...] = logits
    clicks = 1.0 / (1.0 + jnp.exp(-logits))
    click_ref[0] = jnp.broadcast_to(jnp.sum(clicks, axis=1, keepdims=True), click_ref.shape[1:])
    tells = []
    for i in range(1, replicas):
        tells.append(
            pltpu.make_async_remote_copy(
                src_ref=click_ref.at[0],
                dst_ref=click_ref.at[i],
                send_sem=click_send.at[i],
                recv_sem=click_recv.at[i],
                device_id={"replica": lax.rem(rep + i, replicas)},
                device_id_type=MESH,
            )
        )
    for tell in tells:
        tell.start()
    for tell in tells:
        tell.wait()
    total = click_ref[0]
    for i in range(1, replicas):
        total = total + click_ref[i]
    share_ref[...] = (replicas * queries) * clicks / total[:1, :1]


def tail(pooled, weight, cross_down, cross_up, cross_bias, top_bias, out_weight, prior):
    shards, queries, lanes = pooled.shape
    replicas = lax.axis_size("replica")
    feat = cross_down.shape[1]
    padded = -(-queries // LANES) * LANES
    vmem = pl.BlockSpec(memory_space=pltpu.VMEM)
    anywhere = pl.BlockSpec(memory_space=pl.ANY)
    dma = pltpu.SemaphoreType.DMA
    return pl.pallas_call(
        tail_kernel,
        out_shape=(jax.ShapeDtypeStruct((1, queries), F32),) * 2,
        in_specs=[anywhere, anywhere, anywhere, anywhere, vmem, vmem, vmem, vmem],
        out_specs=(vmem, vmem),
        scratch_shapes=[
            pltpu.VMEM((shards, queries, lanes), BF16),
            pltpu.VMEM((queries, feat), BF16),
            pltpu.VMEM((queries, feat), BF16),
            pltpu.VMEM(weight.shape, BF16),
            pltpu.VMEM(cross_down.shape, BF16),
            pltpu.VMEM(cross_up.shape, BF16),
            pltpu.VMEM((8, padded), F32),
            pltpu.VMEM((8, padded), F32),
            pltpu.VMEM((replicas, 8, LANES), F32),
            pltpu.VMEM((padded, LANES), F32),
            dma((shards,)),
            dma((shards,)),
            dma,
            dma((3,)),
            dma,
            dma,
            dma,
            dma,
            dma((replicas,)),
            dma((replicas,)),
        ],
        compiler_params=pltpu.CompilerParams(
            collective_id=1, has_side_effects=True, vmem_limit_bytes=56 * 2**20
        ),
        cost_estimate=pl.CostEstimate(flops=int(20e9), bytes_accessed=24000000, transcendentals=0),
        name="tail",
    )(pooled, weight, cross_down, cross_up, cross_bias, top_bias, out_weight, prior)


def body(
    core_first,
    core_middle,
    core_last,
    idx_first,
    idx_middle,
    idx_last,
    bag_lengths,
    cross_down,
    cross_up,
    cross_bias,
    top_weight,
    top_bias,
    out_weight,
    prior,
):
    shards = lax.axis_size("tables")
    queries = idx_first.shape[2]

    core = lax.rem(lax.axis_index("replica"), 2)
    half = top_weight.shape[1] // 2
    part = lax.dynamic_slice_in_dim(top_weight, core * half, half, axis=1)
    weight = lax.all_gather(part, "tables", axis=0)

    def my_units(values):
        return lax.dynamic_index_in_dim(values.reshape(shards, 2, half), core, 1, keepdims=False)

    in_bag = jnp.arange(BAG, dtype=I32)[None, :, None] < bag_lengths[0, 0].T[:, None, :]

    def by_table(values):
        return jnp.transpose(values[0, 0], (1, 2, 0))

    sent = jnp.concatenate(
        [
            by_table(idx_first),
            by_table(idx_middle),
            jnp.where(in_bag, by_table(idx_last), -1),
        ],
        axis=1,
    )
    at_owner = lax.all_to_all(sent, "tables", split_axis=0, concat_axis=0, tiled=True)
    at_owner = jnp.transpose(at_owner, (1, 0, 2))
    first_ids, middle_ids, last_ids = (
        at_owner[BAG * i : BAG * (i + 1)].reshape(-1, LANES) for i in range(3)
    )
    dest, owner, slot = order(first_ids, middle_ids, core_middle.shape[1])
    pooled = lookup(
        dest, owner, slot, last_ids.T, core_first[0], core_middle[0], core_last[0]
    )
    logits, click_share = tail(
        pooled.reshape(shards, queries, LANES),
        weight,
        cross_down,
        cross_up,
        cross_bias,
        my_units(top_bias).astype(F32),
        my_units(out_weight).astype(F32),
        prior[0],
    )
    return (logits[None], click_share[None])


def solution(mesh):
    in_specs = (
        P("tables", None, None),
        P("tables", None, None, None),
        P("tables", None, None),
        P("replica", "tables", None, None, None),
        P("replica", "tables", None, None, None),
        P("replica", "tables", None, None, None),
        P("replica", "tables", None, None),
        P(),
        P(),
        P(),
        P(None, "tables"),
        P(),
        P(),
        P("replica", "tables", None),
    )
    out_specs = (P("replica", "tables", None), P("replica", "tables", None))
    return jax.shard_map(body, mesh=mesh, in_specs=in_specs, out_specs=out_specs, check_vma=False)
```

time: 321 us -> 149 us (0.46)
  waiting for transfers between devices: 92 us -> 5.96 us
  Pallas kernels: 169 us -> 109 us
  blocking collectives: 28.3 us -> 0 us
    all_gather x1, waiting for transfers between devices: 74.7 us -> 0.01 us  [body(): weight = lax.all_gather(part, 'tables', axis=0)]
    pallas_call x1, Pallas kernels: 128 us -> 62.4 us  [lookup(): pl.pallas_call(functools.partial(lookup_kernel, items), out_shape=jax.Sha...]
    pallas_call x1, Pallas kernels: 20.2 us -> 40.4 us  [tail(): pl.pallas_call(tail_kernel, out_shape=(jax.ShapeDtypeStruct((1, queries),...]
    psum x1 -> x0, blocking collectives: 15.8 us -> none  [body(): request_sum = lax.psum(jnp.sum(clicks), 'replica')]
    pallas_call x1, Pallas kernels: 20.2 us -> 6.41 us  [order(): pl.pallas_call(functools.partial(order_kernel, groups), out_shape=(jax.Sh...]
    all_to_all x1 -> x0, blocking collectives: 12.6 us -> none  [body(): lax.all_to_all(sent, 'tables', split_axis=0, concat_axis=0, tiled=True)]
    all_to_all x1, waiting for transfers between devices: 17.3 us -> 5.94 us  [body(): lax.all_to_all(sent, 'tables', split_axis=0, concat_axis=0, tiled=True)]
    all_to_all x1, starting transfers between devices: 3.84 us -> 7.58 us  [body(): lax.all_to_all(sent, 'tables', split_axis=0, concat_axis=0, tiled=True)]
  transfers between devices with their start and end apart: 3 -> 2, of which waited for: 2 -> 1; matrix products, arithmetic and copies ran while one was open for 2% -> 5% of each run, Pallas kernels for 46% -> 46%
where the time goes in v2:
time: 149 us
  Pallas kernels  109 us (73%)
  between operations  14.1 us (9%)
  local copies, waits for them, and re-layouts  8.17 us (5%)
  starting transfers between devices  7.62 us (5%)
  waiting for transfers between devices  5.96 us (4%)
  other arithmetic  3.61 us (2%)
    pallas_call x1, Pallas kernels, lookup(): pl.pallas_call(functools.partial(lookup_kernel, items), out_shape=jax.Sha...  62.4 us
    pallas_call x1, Pallas kernels, tail(): pl.pallas_call(tail_kernel, out_shape=(jax.ShapeDtypeStruct((1, queries),...  40.4 us
    all_to_all x1, starting transfers between devices, body(): lax.all_to_all(sent, 'tables', split_axis=0, concat_axis=0, tiled=True)  7.58 us
    pallas_call x1, Pallas kernels, order(): pl.pallas_call(functools.partial(order_kernel, groups), out_shape=(jax.Sh...  6.41 us
    all_to_all x1, waiting for transfers between devices, body(): lax.all_to_all(sent, 'tables', split_axis=0, concat_axis=0, tiled=True)  5.94 us
    unnamed x9, local copies, waits for them, and re-layouts  5.04 us
  transfers between devices with their start and end apart: 2, of which 1 were waited for; matrix products, arithmetic and copies ran while one was open for 5% of the time, Pallas kernels for 46%

profile of v2, /device:TPU:1, one launch (start us, length us, event | category | flops | bytes accessed | tf_op | source)
XLA Modules:
  0.0 148.7 jit_solution(1516341828107627445)
XLA Ops:
  7.2 0.0 copy-start
  7.2 0.0 copy-start.1
  7.2 0.0 copy-start.2
  7.2 0.0 all-gather.3.cloned.1.call-start
  7.3 1.1 copy-done
  8.4 0.8 constant_dynamic-slice_fusion.2
  9.2 0.0 all-gather.3.cloned.1.call-update
  9.3 0.8 compare_select_fusion
  10.1 1.6 %pad_add_fusion = s32[16,6,320]{2,1,0:T(8,128)} fusion(s32[16,2,320]{2,1,0:T(2,128)S(1)} %compare_select_fusion, s32[16,2,320]{2,1,0:T(2,128)} %bitcast.39, s32[16,2,320]{2,1,0:T(2,128)} %bitcast.40), kind=kLoop, calls=%fused_computation | loop fusion | flops 61440 | bytes 245760 | tf_op jit(solution)/shard_map/concatenate | solution.py:505
  11.7 7.6 %all-to-all-start = ((s32[16,6,320]{2,1,0:T(8,128)}), s32[16,6,320]{2,1,0:T(8,128)S(1)}, u32[]{:S(2)}, u32[]{:S(2)}) async-start(s32[16,6,320]{2,1,0:T(8,128)} %pad_add_fusion), calls=%async_computation | async-start | bytes 393216 | tf_op jit(solution)/shard_map/all_to_all | solution.py:513
  19.3 0.0 copy-done.1
  19.3 0.0 copy-done.2
  19.3 0.6 fusion.out_weight_ref
  19.9 0.6 fusion.1.top_bias_ref
  20.5 5.9 %all-to-all-done = s32[16,6,320]{2,1,0:T(8,128)S(1)} async-done(((s32[16,6,320]{2,1,0:T(8,128)}), s32[16,6,320]{2,1,0:T(8,128)S(1)}, u32[]{:S(2)}, u32[]{:S(2)}) %all-to-all-start) | async-done | bytes 122912 | tf_op jit(solution)/shard_map/all_to_all | solution.py:513
  26.5 0.1 fusion.2
  26.5 0.1 reshape.25
  26.6 0.7 copy.21
  27.3 0.7 reshape_reshape.7.middle_ref
  28.0 0.7 reshape_reshape.6.first_ref
  28.8 6.4 %order.1 = (s32[40,256]{1,0:T(8,128)}, s32[1,512]{1,0:T(1,128)}, s32[128,128]{1,0:T(8,128)}) custom-call(s32[40,256]{1,0:T(8,128)} %reshape_reshape.6.first_ref, s32[40,256]{1,0:T(8,128)} %reshape_reshape.7.middle_ref), custom_call_target="tpu_custom_call" | custom-call | flops 2000000000 | bytes 200000 | tf_op jit(solution)/shard_map/order/pallas_call | solution.py:103
  35.2 1.4 copy.26
  36.6 62.4 %lookup.1 = bf16[5120,128]{1,0:T(8,128)(2,1)} custom-call(s32[10240]{0:T(1024)} %bitcast.42, s32[1,512]{1,0:T(1,128)} %get-tuple-element.8.owner_ref, s32[128,128]{1,0:T(8,128)} %get-tuple-element.9.slot_ref, s32[128,80]{1,0:T(8,128)} %bitcast.38, bf16[512,512]{1,0:T(8,128)(2,1)} %bitcast.50, bf16[80,64,128]{2,1,0:T(8,128)(2,1)} %bitcast.49, ...), custom_call_target="tpu_custom_call" | custom-call | flops 60000002048 | bytes 5000000 | tf_op jit(solution)/shard_map/lookup/pallas_call | solution.py:286
  99.0 0.0 all-gather.3.cloned.1.call-done
  99.0 40.4 %tail.1 = (f32[1,320]{1,0:T(1,128)}, f32[1,320]{1,0:T(1,128)}) custom-call(bf16[16,320,128]{2,1,0:T(8,128)(2,1)} %bitcast.53, bf16[16,2048,128]{2,1,0:T(8,128)(2,1)} %bitcast.48, bf16[2,2048,256]{2,1,0:T(8,128)(2,1)} %down_ref.1, bf16[2,256,2048]{2,1,0:T(8,128)(2,1)} %up_ref.1, bf16[2,2048]{1,0:T(2,128)(2,1)} %bias_ref.1, f32[16,128]{1,0:T(8,128)} %fusion.1.top_bias_ref, ...), custom_call_target="tpu_custom_call" | custom-call | flops 20000000000 | bytes 24000000 | tf_op jit(solution)/shard_map/tail/pallas_call | solution.py:438
  139.4 1.2 copy.35
  140.6 1.2 copy.36
  (4 shorter events, 0.0 us)
Async XLA Ops:
  7.2 1.2 copy-start
  7.2 12.1 %copy-start.1 = (bf16[4096]{0:T(1024)(128)(2,1)S(1)}, bf16[4096]{0:T(1024)(128)(2,1)}, u32[]{:S(2)}) copy-start(bf16[4096]{0:T(1024)(128)(2,1)} %param.26) | copy-start | bytes 24580
  7.2 12.1 %copy-start.2 = (bf16[4096]{0:T(1024)(128)(2,1)S(1)}, bf16[4096]{0:T(1024)(128)(2,1)}, u32[]{:S(2)}) copy-start(bf16[4096]{0:T(1024)(128)(2,1)} %param.25) | copy-start | bytes 24580
  7.2 91.8 %all-gather.3.cloned.1.call-start = ((), (), s32[]{:S(2)}) async-start(), calls=%async_computation.1 | async-start | bytes 8912896 | tf_op jit(solution)/shard_map/all_gather | solution.py:495
  11.7 14.8 %all-to-all-start = ((s32[16,6,320]{2,1,0:T(8,128)}), s32[16,6,320]{2,1,0:T(8,128)S(1)}, u32[]{:S(2)}, u32[]{:S(2)}) async-start(s32[16,6,320]{2,1,0:T(8,128)} %pad_add_fusion), calls=%async_computation | async-start | bytes 393216 | tf_op jit(solution)/shard_map/all_to_all | solution.py:513
Sparse Core Ops, SparseCore 0:
  10.2 73.8 all-gather.2

commit v3 on v2

--- a/solution.py
+++ b/solution.py
@@ -116,29 +116,38 @@
     )(first_ids.reshape(-1, width), middle_ids.reshape(-1, width))
 
 
-def lookup_kernel(
+def main_kernel(
     items,
-    dest_ref,
-    owner_ref,
-    slot_ref,
-    last_ids_ref,
-    first_ref,
-    middle_ref,
-    last_ref,
-    out_ref,
-    pair_ref,
-    last_by_d3_ref,
-    left_ref,
-    spread_ref,
-    cores_a_ref,
-    cores_b_ref,
-    last_a_ref,
-    last_b_ref,
-    staged_ref,
-    diag_a_ref,
-    diag_b_ref,
-    gather_own_ref,
+    dest_ref, owner_ref, slot_ref, last_ids_ref, first_ref, middle_ref, last_ref,
+    weight_ref, down_ref, up_ref, bias_ref, top_bias_ref, out_weight_ref, prior_ref,
+    both_ref,
+    pair_ref, last_by_d3_ref, left_ref, spread_ref, cores_a_ref, cores_b_ref, last_a_ref, last_b_ref,
+    staged_ref, diag_a_ref, diag_b_ref, gather_own_ref,
+    out_ref, recv_ref, mine_ref, theirs_ref, down_v, up_v, part_ref, part_in_ref, click_ref, sum_ref,
+    pooled_send, pooled_recv, weight_sem, pair_send, pair_recv, part_send, part_recv,
+    click_send, click_recv,
 ):
+    shards, mine, lanes = recv_ref.shape
+    replicas = lax.axis_size("replica")
+    me, rep = lax.axis_index("tables"), lax.axis_index("replica")
+    sibling = rep + 1 - 2 * lax.rem(rep, 2)
+    barrier = pltpu.get_barrier_semaphore()
+    for i in range(1, shards):
+        pl.semaphore_signal(
+            barrier, inc=1, device_id={"tables": lax.rem(me + i, shards)}, device_id_type=MESH
+        )
+    for i in range(1, replicas):
+        pl.semaphore_signal(
+            barrier, inc=1, device_id={"replica": lax.rem(rep + i, replicas)}, device_id_type=MESH
+        )
+    fetches = [
+        pltpu.make_async_copy(down_ref, down_v, weight_sem.at[0]),
+        pltpu.make_async_copy(up_ref, up_v, weight_sem.at[1]),
+        pltpu.make_async_copy(weight_ref, left_ref.at[pl.ds(0, weight_ref.shape[0])], weight_sem.at[2]),
+    ]
+    fetches[0].start()
+    fetches[1].start()
+
     queries = items // BAG
     groups, rank, wide = middle_ref.shape
     rows, first_width = first_ref.shape
@@ -161,10 +170,9 @@
     per_step = STEP // TILE
     pairs = left_ref.shape[0] // (2 * STEP)
     slot_lane = iota((LANES, LANES), 1)
-    row_lane = iota((LANES, rows), 1)
 
     def hot_of(ids):
-        return (row_lane == ids).astype(F32).astype(BF16)
+        return (iota((ids.shape[0], rows), 1) == ids).astype(F32).astype(BF16)
 
     def gather_first(step, to_ref):
         hots = []
@@ -209,8 +217,9 @@
     lax.fori_loop(0, pairs, left_pair, 0)
 
     group = TILE
-    per_block = LANES // group
-    blocks = queries // LANES
+    unit = last_ids_ref.shape[0]
+    units = mine // unit
+    per_unit = unit // group
     id_lane = iota(last_ids_ref.shape, 1)
     low_half = iota((group, LANES), 1) < rank
     own = (iota((group, LANES), 1) >> 3) == (iota((group, LANES), 0) & 15)
@@ -218,19 +227,19 @@
     tap, spot = iota((taps, LANES), 0), iota((taps, LANES), 1)
     gather_own_ref[...] = (spot == (tap & (D1 - 1)) * (D2 * D3) + (tap >> 7)).astype(F32).astype(BF16)
 
-    def gather_last(block, to_ref):
+    def gather_last(number, to_ref):
         hots = [
             hot_of(
                 jnp.sum(
-                    jnp.where(id_lane == k * blocks + block, last_ids_ref[...], 0), axis=1, keepdims=True
+                    jnp.where(id_lane == k * shards * units + number, last_ids_ref[...], 0), axis=1, keepdims=True
                 )
             )
             for k in range(BAG)
         ]
         to_ref[...] = dot(jnp.concatenate(hots, axis=0), last_by_d3_ref[...])
 
-    def make_group(block, part, which, from_ref, diag_ref):
-        base = block * LANES + part * group
+    def make_group(number, part, which, from_ref, diag_ref):
+        base = number * unit + part * group
         for k in range(BAG):
             for q in range(group):
                 at = dest_ref[k * queries + base + q]
@@ -240,7 +249,7 @@
         )
         pieces = [[None] * BAG for _ in range(D2 * D3)]
         for k in range(BAG):
-            start = k * LANES + part * group
+            start = k * unit + part * group
             for tile in range(D3 // 2):
                 both = from_ref[start : start + group, tile * LANES : (tile + 1) * LANES]
                 low = jnp.where(low_half, both, 0.0)
@@ -260,105 +269,45 @@
                 own, mine, 0.0
             ).astype(BF16)
 
-    def make_block(block, which, from_ref, diag_ref):
-        for part in range(per_block):
-            make_group(block, part, which + part, from_ref, diag_ref)
-        out_ref[pl.ds(block * LANES, LANES), :] = dot(diag_ref[...], gather_own_ref[...]).astype(BF16)
-
-    gather_last(0, last_a_ref)
-
-    def block_pair(pair, carry):
-        gather_last(2 * pair + 1, last_b_ref)
-        make_block(2 * pair, 0, last_a_ref, diag_a_ref)
-        gather_last(jnp.minimum(2 * pair + 2, blocks - 1), last_a_ref)
-        make_block(2 * pair + 1, per_block, last_b_ref, diag_b_ref)
+    def make_unit(to, number, from_ref, diag_ref):
+        for part in range(per_unit):
+            make_group(to * units + number, part, number * per_unit + part, from_ref, diag_ref)
+        out_ref[to, number * unit : (number + 1) * unit, :] = dot(
+            diag_ref[...], gather_own_ref[...]
+        ).astype(BF16)
+
+    def send_of(i):
+        to = lax.rem(me + 1 + i, shards)
+        return pltpu.make_async_remote_copy(
+            src_ref=out_ref.at[to],
+            dst_ref=recv_ref.at[me],
+            send_sem=pooled_send.at[i],
+            recv_sem=pooled_recv.at[i],
+            device_id={"tables": to},
+            device_id_type=MESH,
+        )
+
+    gather_last(lax.rem(me + 1, shards) * units, last_a_ref)
+    pl.semaphore_wait(barrier, shards + replicas - 2)
+
+    def make_owner(i, carry):
+        to, after = lax.rem(me + 1 + i, shards), lax.rem(me + 2 + i, shards)
+        gather_last(to * units + 1, last_b_ref)
+        make_unit(to, 0, last_a_ref, diag_a_ref)
+        gather_last(after * units, last_a_ref)
+        make_unit(to, 1, last_b_ref, diag_b_ref)
+
+        @pl.when(i < shards - 1)
+        def _():
+            send_of(i).start()
+
         return carry
 
-    lax.fori_loop(0, blocks // 2, block_pair, 0)
-
-
-def lookup(dest, owner, slot, last_ids, core_first, core_middle, core_last):
-    items = dest.size
-    groups, rank, wide = core_middle.shape
-    slots = -(-(items + groups * TILE) // (2 * STEP)) * 2 * STEP
-    smem = pl.BlockSpec(memory_space=pltpu.SMEM)
-    vmem = pl.BlockSpec(memory_space=pltpu.VMEM)
-    return pl.pallas_call(
-        functools.partial(lookup_kernel, items),
-        out_shape=jax.ShapeDtypeStruct((items // BAG, LANES), BF16),
-        in_specs=[smem, smem, vmem, vmem, vmem, vmem, vmem],
-        out_specs=vmem,
-        scratch_shapes=[
-            pltpu.VMEM((groups, 2 * rank, 2 * wide), BF16),
-            pltpu.VMEM(core_last.shape, BF16),
-            pltpu.VMEM((slots, D1, wide), BF16),
-            pltpu.VMEM((STEP // TILE, TILE * D1, wide), F32),
-            pltpu.VMEM((STEP, core_first.shape[1]), BF16),
-            pltpu.VMEM((STEP, core_first.shape[1]), BF16),
-            pltpu.VMEM((BAG * LANES, core_last.shape[1]), F32),
-            pltpu.VMEM((BAG * LANES, core_last.shape[1]), F32),
-            pltpu.VMEM((2 * LANES // TILE, BAG, TILE, D1, wide), BF16),
-            pltpu.VMEM((LANES, D2 * D3 * LANES), BF16),
-            pltpu.VMEM((LANES, D2 * D3 * LANES), BF16),
-            pltpu.VMEM((D2 * D3 * LANES, LANES), BF16),
-        ],
-        compiler_params=pltpu.CompilerParams(vmem_limit_bytes=56 * 2**20),
-        cost_estimate=pl.CostEstimate(flops=int(60e9), bytes_accessed=5000000, transcendentals=0),
-        name="lookup",
-    )(dest.reshape(-1), owner, slot, last_ids, core_first, core_middle, core_last)
-
-
-def tail_kernel(
-    pooled_ref, weight_ref, down_ref, up_ref, bias_ref, top_bias_ref, out_weight_ref, prior_ref,
-    logit_ref, share_ref,
-    recv_ref, mine_ref, theirs_ref, wide_ref, down_v, up_v, part_ref, part_in_ref, click_ref, sum_ref,
-    pooled_send, pooled_recv, local_sem, weight_sem, pair_send, pair_recv, part_send, part_recv,
-    click_send, click_recv,
-):
-    shards, queries, lanes = pooled_ref.shape
-    replicas = lax.axis_size("replica")
-    me, rep = lax.axis_index("tables"), lax.axis_index("replica")
-    sibling = rep + 1 - 2 * lax.rem(rep, 2)
-
-    fetches = [
-        pltpu.make_async_copy(down_ref, down_v, weight_sem.at[0]),
-        pltpu.make_async_copy(up_ref, up_v, weight_sem.at[1]),
-        pltpu.make_async_copy(weight_ref, wide_ref, weight_sem.at[2]),
-    ]
-    for fetch in fetches:
-        fetch.start()
-    keep = pltpu.make_async_copy(pooled_ref.at[me], recv_ref.at[me], local_sem)
-    keep.start()
-
-    barrier = pltpu.get_barrier_semaphore()
-    for i in range(1, shards):
-        pl.semaphore_signal(
-            barrier, inc=1, device_id={"tables": lax.rem(me + i, shards)}, device_id_type=MESH
-        )
-    for i in range(1, replicas):
-        pl.semaphore_signal(
-            barrier, inc=1, device_id={"replica": lax.rem(rep + i, replicas)}, device_id_type=MESH
-        )
-    pl.semaphore_wait(barrier, shards + replicas - 2)
-
-    sends = []
-    for i in range(1, shards):
-        to = lax.rem(me + i, shards)
-        sends.append(
-            pltpu.make_async_remote_copy(
-                src_ref=pooled_ref.at[to],
-                dst_ref=recv_ref.at[me],
-                send_sem=pooled_send.at[i],
-                recv_sem=pooled_recv.at[i],
-                device_id={"tables": to},
-                device_id_type=MESH,
-            )
-        )
-    for send in sends:
-        send.start()
-    keep.wait()
-    for send in sends:
-        send.wait()
+    lax.fori_loop(0, shards, make_owner, 0)
+    fetches[2].start()
+    recv_ref[me] = out_ref[me]
+    for i in range(shards - 1):
+        send_of(i).wait()
     fetches[0].wait()
     fetches[1].wait()
 
@@ -380,13 +329,16 @@
         sum_ref[...] = jnp.zeros_like(sum_ref)
 
         def step(t, carry):
-            weight = jnp.concatenate([wide_ref[2 * t], wide_ref[2 * t + 1]], axis=1)
+            span = down_v.shape[1] // D1
+            weight = jnp.concatenate(
+                [left_ref[pl.ds((2 * t + h) * span, span)].reshape(span * D1, lanes) for h in range(2)], axis=1
+            )
             hidden = dot(rows_ref[...], weight)
             for half in range(2):
                 at = 2 * t + half
                 unit = hidden[:, half * lanes : (half + 1) * lanes] + top_bias_ref[pl.ds(at, 1), :]
                 unit = jnp.maximum(unit, 0.0).astype(BF16).astype(F32)
-                sum_ref[:queries] += unit * out_weight_ref[pl.ds(at, 1), :]
+                sum_ref[:mine] += unit * out_weight_ref[pl.ds(at, 1), :]
             return carry
 
         lax.fori_loop(0, shards // 2, step, 0)
@@ -401,8 +353,8 @@
     )
     back.start()
     back.wait()
-    logits = (ours + part_in_ref[:1])[:, :queries] + prior_ref[...]
-    logit_ref[...] = logits
+    logits = (ours + part_in_ref[:1])[:, :mine] + prior_ref[...]
+    both_ref[:1] = logits
     clicks = 1.0 / (1.0 + jnp.exp(-logits))
     click_ref[0] = jnp.broadcast_to(jnp.sum(clicks, axis=1, keepdims=True), click_ref.shape[1:])
     tells = []
@@ -424,27 +376,47 @@
     total = click_ref[0]
     for i in range(1, replicas):
         total = total + click_ref[i]
-    share_ref[...] = (replicas * queries) * clicks / total[:1, :1]
-
-
-def tail(pooled, weight, cross_down, cross_up, cross_bias, top_bias, out_weight, prior):
-    shards, queries, lanes = pooled.shape
-    replicas = lax.axis_size("replica")
+    both_ref[1:] = (replicas * mine) * clicks / total[:1, :1]
+
+
+def main(
+    dest, owner, slot, last_ids, core_first, core_middle, core_last,
+    weight, cross_down, cross_up, cross_bias, top_bias, out_weight, prior,
+):
+    items = dest.size
+    groups, rank, wide = core_middle.shape
+    slots = -(-(items + groups * TILE) // (2 * STEP)) * 2 * STEP
+    shards, replicas = lax.axis_size("tables"), lax.axis_size("replica")
+    queries = prior.shape[1]
     feat = cross_down.shape[1]
     padded = -(-queries // LANES) * LANES
+    unit = last_ids.shape[0]
+    smem = pl.BlockSpec(memory_space=pltpu.SMEM)
     vmem = pl.BlockSpec(memory_space=pltpu.VMEM)
     anywhere = pl.BlockSpec(memory_space=pl.ANY)
     dma = pltpu.SemaphoreType.DMA
     return pl.pallas_call(
-        tail_kernel,
-        out_shape=(jax.ShapeDtypeStruct((1, queries), F32),) * 2,
-        in_specs=[anywhere, anywhere, anywhere, anywhere, vmem, vmem, vmem, vmem],
-        out_specs=(vmem, vmem),
+        functools.partial(main_kernel, items),
+        out_shape=jax.ShapeDtypeStruct((2, queries), F32),
+        in_specs=[smem, smem, vmem, vmem, vmem, vmem, vmem, anywhere, anywhere, anywhere, vmem, vmem, vmem, vmem],
+        out_specs=vmem,
         scratch_shapes=[
-            pltpu.VMEM((shards, queries, lanes), BF16),
+            pltpu.VMEM((groups, 2 * rank, 2 * wide), BF16),
+            pltpu.VMEM(core_last.shape, BF16),
+            pltpu.VMEM((slots, D1, wide), BF16),
+            pltpu.VMEM((STEP // TILE, TILE * D1, wide), F32),
+            pltpu.VMEM((STEP, core_first.shape[1]), BF16),
+            pltpu.VMEM((STEP, core_first.shape[1]), BF16),
+            pltpu.VMEM((BAG * unit, core_last.shape[1]), F32),
+            pltpu.VMEM((BAG * unit, core_last.shape[1]), F32),
+            pltpu.VMEM((queries // TILE, BAG, TILE, D1, wide), BF16),
+            pltpu.VMEM((unit, D2 * D3 * LANES), BF16),
+            pltpu.VMEM((unit, D2 * D3 * LANES), BF16),
+            pltpu.VMEM((D2 * D3 * LANES, LANES), BF16),
+            pltpu.VMEM((shards, queries, LANES), BF16),
+            pltpu.VMEM((shards, queries, LANES), BF16),
             pltpu.VMEM((queries, feat), BF16),
             pltpu.VMEM((queries, feat), BF16),
-            pltpu.VMEM(weight.shape, BF16),
             pltpu.VMEM(cross_down.shape, BF16),
             pltpu.VMEM(cross_up.shape, BF16),
             pltpu.VMEM((8, padded), F32),
@@ -453,7 +425,6 @@
             pltpu.VMEM((padded, LANES), F32),
             dma((shards,)),
             dma((shards,)),
-            dma,
             dma((3,)),
             dma,
             dma,
@@ -463,11 +434,14 @@
             dma((replicas,)),
         ],
         compiler_params=pltpu.CompilerParams(
-            collective_id=1, has_side_effects=True, vmem_limit_bytes=56 * 2**20
+            collective_id=1, has_side_effects=True, vmem_limit_bytes=60 * 2**20
         ),
-        cost_estimate=pl.CostEstimate(flops=int(20e9), bytes_accessed=24000000, transcendentals=0),
-        name="tail",
-    )(pooled, weight, cross_down, cross_up, cross_bias, top_bias, out_weight, prior)
+        cost_estimate=pl.CostEstimate(flops=int(100e9), bytes_accessed=24000000, transcendentals=0),
+        name="main",
+    )(
+        dest.reshape(-1), owner, slot, last_ids, core_first, core_middle, core_last,
+        weight.reshape(-1, D1, LANES), cross_down, cross_up, cross_bias, top_bias, out_weight, prior,
+    )
 
 
 def body(
@@ -516,11 +490,15 @@
         at_owner[BAG * i : BAG * (i + 1)].reshape(-1, LANES) for i in range(3)
     )
     dest, owner, slot = order(first_ids, middle_ids, core_middle.shape[1])
-    pooled = lookup(
-        dest, owner, slot, last_ids.T, core_first[0], core_middle[0], core_last[0]
-    )
-    logits, click_share = tail(
-        pooled.reshape(shards, queries, LANES),
+    unit = queries // 2
+    both = main(
+        dest,
+        owner,
+        slot,
+        last_ids.reshape(-1, unit).T,
+        core_first[0],
+        core_middle[0],
+        core_last[0],
         weight,
         cross_down,
         cross_up,
@@ -529,7 +507,7 @@
         my_units(out_weight).astype(F32),
         prior[0],
     )
-    return (logits[None], click_share[None])
+    return (both[:1][None], both[1:][None])
 
 
 def solution(mesh):

time: 149 us -> 174 us (1.17)
  waiting for transfers between devices: 5.96 us -> 53.6 us
  Pallas kernels: 109 us -> 87.4 us
    all_gather x1, waiting for transfers between devices: 0.01 us -> 47.6 us  [body(): weight = lax.all_gather(part, 'tables', axis=0)]
    pallas_call x2 -> x1, Pallas kernels: 103 us -> 81 us  [main(): pl.pallas_call(functools.partial(main_kernel, items), out_shape=jax.Shape...]
    unnamed x9 -> x7, local copies, waits for them, and re-layouts: 5.04 us -> 2.57 us
  transfers between devices with their start and end apart: 2 -> 2, of which waited for: 1 -> 2; matrix products, arithmetic and copies ran while one was open for 5% -> 4% of each run, Pallas kernels for 46% -> 4%
where the time goes in v3:
time: 174 us; the launch traced here: 173 us
  Pallas kernels  87.4 us (50%)
  waiting for transfers between devices  53.6 us (31%)
  between operations  14.1 us (8%)
  starting transfers between devices  7.62 us (4%)
  local copies, waits for them, and re-layouts  7.06 us (4%)
  other arithmetic  3.6 us (2%)
    pallas_call x1, Pallas kernels, main(): pl.pallas_call(functools.partial(main_kernel, items), out_shape=jax.Shape...  81 us
    all_gather x1, waiting for transfers between devices, body(): weight = lax.all_gather(part, 'tables', axis=0)  47.6 us
    all_to_all x1, starting transfers between devices, body(): lax.all_to_all(sent, 'tables', split_axis=0, concat_axis=0, tiled=True)  7.58 us
    pallas_call x1, Pallas kernels, order(): pl.pallas_call(functools.partial(order_kernel, groups), out_shape=(jax.Sh...  6.41 us
    all_to_all x1, waiting for transfers between devices, body(): lax.all_to_all(sent, 'tables', split_axis=0, concat_axis=0, tiled=True)  5.94 us
  transfers between devices with their start and end apart: 2, of which 2 were waited for; matrix products, arithmetic and copies ran while one was open for 4% of the time, Pallas kernels for 4%

profile of v3, /device:TPU:1, one launch (start us, length us, event | category | flops | bytes accessed | tf_op | source)
XLA Modules:
  0.0 173.3 jit_solution(7125463516219391746)
XLA Ops:
  7.2 0.0 copy-start
  7.2 0.0 copy-start.2
  7.2 0.0 copy-start.1
  7.2 0.0 all-gather.3.cloned.1.call-start
  7.3 1.1 copy-done
  8.4 0.9 constant_dynamic-slice_fusion.2
  9.3 0.0 all-gather.3.cloned.1.call-update
  9.3 0.8 compare_select_fusion
  10.1 1.6 pad_add_fusion
  11.7 7.6 %all-to-all-start = ((s32[16,6,320]{2,1,0:T(8,128)}), s32[16,6,320]{2,1,0:T(8,128)S(1)}, u32[]{:S(2)}, u32[]{:S(2)}) async-start(s32[16,6,320]{2,1,0:T(8,128)} %pad_add_fusion), calls=%async_computation | async-start | bytes 393216 | tf_op jit(solution)/shard_map/all_to_all | solution.py:487
  19.3 0.0 copy-done.2
  19.3 0.0 copy-done.1
  19.3 0.6 fusion.out_weight_ref
  19.9 0.6 fusion.1.top_bias_ref
  20.5 5.9 %all-to-all-done = s32[16,6,320]{2,1,0:T(8,128)S(1)} async-done(((s32[16,6,320]{2,1,0:T(8,128)}), s32[16,6,320]{2,1,0:T(8,128)S(1)}, u32[]{:S(2)}, u32[]{:S(2)}) %all-to-all-start) | async-done | bytes 122912 | tf_op jit(solution)/shard_map/all_to_all | solution.py:487
  26.5 0.1 fusion.2
  26.5 0.7 reshape_reshape.10.middle_ref
  27.3 0.7 reshape_reshape.9.first_ref
  28.0 6.4 %order.1 = (s32[40,256]{1,0:T(8,128)}, s32[1,512]{1,0:T(1,128)}, s32[128,128]{1,0:T(8,128)}) custom-call(s32[40,256]{1,0:T(8,128)} %reshape_reshape.9.first_ref, s32[40,256]{1,0:T(8,128)} %reshape_reshape.10.middle_ref), custom_call_target="tpu_custom_call" | custom-call | flops 2000000000 | bytes 200000 | tf_op jit(solution)/shard_map/order/pallas_call | solution.py:103
  34.4 1.4 copy.26
  35.8 0.1 reshape_reshape.11
  35.9 0.7 copy.21
  36.6 47.6 %all-gather.3.cloned.1.call-done = bf16[32768,128]{1,0:T(8,128)(2,1)} async-done(((bf16[2048,128]{1,0:T(8,128)(2,1)}), bf16[32768,128]{1,0:T(8,128)(2,1)}) %all-gather.3.cloned.1.call-update) | async-done | bytes 8388624 | tf_op jit(solution)/shard_map/all_gather | solution.py:469
  84.2 81.0 %main.1 = f32[2,320]{1,0:T(2,128)} custom-call(s32[10240]{0:T(1024)} %bitcast.42, s32[1,512]{1,0:T(1,128)} %get-tuple-element.6.owner_ref, s32[128,128]{1,0:T(8,128)} %get-tuple-element.7.slot_ref, s32[160,64]{1,0:T(8,128)} %bitcast.39, bf16[512,512]{1,0:T(8,128)(2,1)} %bitcast.49, bf16[80,64,128]{2,1,0:T(8,128)(2,1)} %bitcast.48, ...), custom_call_target="tpu_custom_call" | custom-call | flops 99999997952 | bytes 24000000 | tf_op jit(solution)/shard_map/main/pallas_call | solution.py:398
  165.2 1.3 slice_bitcast_fusion
  (4 shorter events, 0.0 us)
Async XLA Ops:
  7.2 1.2 copy-start
  7.2 12.1 %copy-start.2 = (bf16[4096]{0:T(1024)(128)(2,1)S(1)}, bf16[4096]{0:T(1024)(128)(2,1)}, u32[]{:S(2)}) copy-start(bf16[4096]{0:T(1024)(128)(2,1)} %param.25) | copy-start | bytes 24580
  7.2 12.1 %copy-start.1 = (bf16[4096]{0:T(1024)(128)(2,1)S(1)}, bf16[4096]{0:T(1024)(128)(2,1)}, u32[]{:S(2)}) copy-start(bf16[4096]{0:T(1024)(128)(2,1)} %param.26) | copy-start | bytes 24580
  7.2 77.0 %all-gather.3.cloned.1.call-start = ((), (), s32[]{:S(2)}) async-start(), calls=%async_computation.1 | async-start | bytes 8912896 | tf_op jit(solution)/shard_map/all_gather | solution.py:469
  11.7 14.8 %all-to-all-start = ((s32[16,6,320]{2,1,0:T(8,128)}), s32[16,6,320]{2,1,0:T(8,128)S(1)}, u32[]{:S(2)}, u32[]{:S(2)}) async-start(s32[16,6,320]{2,1,0:T(8,128)} %pad_add_fusion), calls=%async_computation | async-start | bytes 393216 | tf_op jit(solution)/shard_map/all_to_all | solution.py:487
Sparse Core Ops, SparseCore 0:
  10.2 73.9 all-gather.2

commit v4 on v3

--- a/solution.py
+++ b/solution.py
@@ -1,5 +1,3 @@
-import functools
-
 import jax
 import jax.numpy as jnp
 from jax import lax
@@ -33,18 +31,25 @@
     return lax.dot_general(a, b, (((1,), (1,)), ((), ())), preferred_element_type=F32)
 
 
-def order_kernel(groups, first_ref, middle_ref, dest_ref, owner_ref, slot_ref, rank_ref, sums_ref):
-    blocks, width = first_ref.shape
+def group_items(groups, got_ref, dest_ref, owner_ref, slot_ref, rank_ref, sums_ref):
+    sources, _, width = got_ref.shape
     group_row = iota((groups, width), 0)
-    before = (iota((width, width), 0) < iota((width, width), 1)).astype(BF16)
+    lane_row = iota((LANES, width), 0)
+    before = (iota((width, width), 0) < iota((width, width), 1)).astype(F32).astype(BF16)
     together = 8
-
-    def hot_rows(first):
-        ids = middle_ref[pl.ds(first, together), :]
-        return [group_row == ids[u : u + 1, :] for u in range(together)]
+    steps = BAG * sources // together
+    per_bag = sources // together
+
+    def rows_of(step, field):
+        rows = []
+        for u in range(together):
+            source = lax.rem(step, per_bag) * together + u
+            at = field * BAG + lax.div(step, per_bag)
+            rows.append(got_ref[source, pl.ds(at, 1), :])
+        return rows
 
     def count(step, seen):
-        hots = hot_rows(step * together)
+        hots = [group_row == row for row in rows_of(step, 1)]
         ones = jnp.concatenate([h.astype(F32) for h in hots], axis=0)
         ranks = dot(ones.astype(BF16), before)
         sizes = jnp.sum(ones, axis=1, keepdims=True)
@@ -53,30 +58,31 @@
             at = slice(u * groups, (u + 1) * groups)
             rows.append(jnp.sum(jnp.where(hots[u], ranks[at] + seen, 0.0), axis=0, keepdims=True))
             seen = seen + sizes[at]
-        rank_ref[pl.ds(step * together, together), :] = jnp.concatenate(rows, axis=0)
+        rank_ref[pl.ds(pl.multiple_of(step * together, together), together), :] = jnp.concatenate(rows, axis=0)
         return seen
 
-    counts = lax.fori_loop(0, blocks // together, count, jnp.zeros((groups, 1), F32))
+    counts = lax.fori_loop(0, steps, count, jnp.zeros((groups, 1), F32))
     tiles = jnp.floor((counts + (TILE - 1)) * (1.0 / TILE))
     tiles = jnp.broadcast_to(tiles, (groups, LANES))
     high = jnp.floor(tiles * (1.0 / 16))
     low = tiles - 16.0 * high
-    above = (iota((groups, groups), 0) > iota((groups, groups), 1)).astype(BF16)
+    above = (iota((groups, groups), 0) > iota((groups, groups), 1)).astype(F32).astype(BF16)
     offset = 16.0 * dot(above, high.astype(BF16)) + dot(above, low.astype(BF16))
     offset = offset[:, :1]
     tile_lane = iota((groups, owner_ref.shape[1]), 1)
-    owner_ref[...] = jnp.sum((offset.astype(I32) <= tile_lane).astype(I32), axis=0, keepdims=True) - 1
-
+    owner_ref[...] = jnp.broadcast_to(
+        jnp.sum((offset.astype(I32) <= tile_lane).astype(I32), axis=0, keepdims=True) - 1, owner_ref.shape
+    )
     sums_ref[...] = jnp.zeros_like(sums_ref)
-    lane_row = iota((LANES, width), 0)
 
     def place(step, carry):
-        first = step * together
-        hots = hot_rows(first)
-        starts = [jnp.sum(jnp.where(h, offset, 0.0), axis=0, keepdims=True) for h in hots]
+        first = pl.multiple_of(step * together, together)
+        middles = rows_of(step, 1)
+        starts = [jnp.sum(jnp.where(group_row == row, offset, 0.0), axis=0, keepdims=True) for row in middles]
         dests = (rank_ref[pl.ds(first, together), :] + TILE * jnp.concatenate(starts, axis=0)).astype(I32)
+        dests = jnp.where(jnp.concatenate(middles, axis=0) < 0, -1, dests)
         dest_ref[pl.ds(first, together), :] = dests
-        ids = first_ref[pl.ds(first, together), :]
+        ids = jnp.concatenate(rows_of(step, 0), axis=0)
         lanes, highs, lows, rows = dests & (LANES - 1), (ids >> 4).astype(F32), (ids & 15).astype(F32), dests >> 7
         values, spots = [], []
         for u in range(together):
@@ -91,39 +97,19 @@
         sums_ref[...] += dot_nt(jnp.concatenate(values, axis=1), jnp.concatenate(spots, axis=1))
         return carry
 
-    lax.fori_loop(0, blocks // together, place, 0)
+    lax.fori_loop(0, steps, place, 0)
     slot_ref[...] = (16.0 * sums_ref[:LANES, :] + sums_ref[LANES:, :]).astype(I32)
 
 
-def order(first_ids, middle_ids, groups):
-    items = first_ids.size
-    width = 256
-    most_tiles = items // TILE + groups
-    owners = -(-most_tiles // LANES) * LANES
-    return pl.pallas_call(
-        functools.partial(order_kernel, groups),
-        out_shape=(
-            jax.ShapeDtypeStruct((items // width, width), I32),
-            jax.ShapeDtypeStruct((1, owners), I32),
-            jax.ShapeDtypeStruct((LANES, LANES), I32),
-        ),
-        scratch_shapes=[
-            pltpu.VMEM((items // width, width), F32),
-            pltpu.VMEM((2 * LANES, LANES), F32),
-        ],
-        cost_estimate=pl.CostEstimate(flops=int(2e9), bytes_accessed=200000, transcendentals=0),
-        name="order",
-    )(first_ids.reshape(-1, width), middle_ids.reshape(-1, width))
-
-
 def main_kernel(
-    items,
-    dest_ref, owner_ref, slot_ref, last_ids_ref, first_ref, middle_ref, last_ref,
-    weight_ref, down_ref, up_ref, bias_ref, top_bias_ref, out_weight_ref, prior_ref,
-    both_ref,
+    idx_first_ref, idx_middle_ref, idx_last_ref, lengths_ref, first_ref, middle_ref, last_ref,
+    top_ref, down_ref, up_ref, bias_ref, units_ref, prior_ref,
+    both_ref, weight_ref,
+    sent_ref, got_ref, last_ids_ref, dest_v, owner_v, slot_ref, rank_ref, places_ref, dest_ref, owner_ref,
     pair_ref, last_by_d3_ref, left_ref, spread_ref, cores_a_ref, cores_b_ref, last_a_ref, last_b_ref,
     staged_ref, diag_a_ref, diag_b_ref, gather_own_ref,
     out_ref, recv_ref, mine_ref, theirs_ref, down_v, up_v, part_ref, part_in_ref, click_ref, sum_ref,
+    ids_send, ids_recv, spread_send, spread_recv, forward_send, forward_recv, local_sem,
     pooled_send, pooled_recv, weight_sem, pair_send, pair_recv, part_send, part_recv,
     click_send, click_recv,
 ):
@@ -140,6 +126,12 @@
         pl.semaphore_signal(
             barrier, inc=1, device_id={"replica": lax.rem(rep + i, replicas)}, device_id_type=MESH
         )
+    core = lax.rem(rep, 2)
+    groups, rank, wide = middle_ref.shape
+    rows = first_ref.shape[0]
+    side = 4 if shards == 16 else 1
+    row, column = lax.div(me, side), lax.rem(me, side)
+    span = down_v.shape[1] // D1
     fetches = [
         pltpu.make_async_copy(down_ref, down_v, weight_sem.at[0]),
         pltpu.make_async_copy(up_ref, up_v, weight_sem.at[1]),
@@ -148,9 +140,66 @@
     fetches[0].start()
     fetches[1].start()
 
-    queries = items // BAG
-    groups, rank, wide = middle_ref.shape
-    rows, first_width = first_ref.shape
+    own_weight = top_ref.at[:, :, pl.ds(pl.multiple_of(core * lanes, lanes), lanes)]
+    half = span // 2
+
+    def shard_part(shard, part):
+        return weight_ref.at[pl.ds(shard * span + part * half, half)]
+
+    keep = pltpu.make_async_copy(own_weight, weight_ref.at[pl.ds(me * span, span)], local_sem)
+    keep.start()
+
+    def spread_of(part, away):
+        to = row * side + lax.rem(column + away, side) if part == 0 else lax.rem(row + away, side) * side + column
+        return pltpu.make_async_remote_copy(
+            src_ref=shard_part(me, part), dst_ref=shard_part(me, part),
+            send_sem=spread_send.at[part, away], recv_sem=spread_recv.at[part, away],
+            device_id={"tables": to}, device_id_type=MESH,
+        )
+
+    def forward_of(part, away, other):
+        if part == 0:
+            shard = row * side + lax.rem(column + other, side)
+            to = lax.rem(row + away, side) * side + column
+        else:
+            shard = lax.rem(row + other, side) * side + column
+            to = row * side + lax.rem(column + away, side)
+        return pltpu.make_async_remote_copy(
+            src_ref=shard_part(shard, part), dst_ref=shard_part(shard, part),
+            send_sem=forward_send.at[part, away, other], recv_sem=forward_recv.at[part, away, other],
+            device_id={"tables": to}, device_id_type=MESH,
+        )
+
+    spreads = [spread_of(part, away) for away in range(1, side) for part in range(2)]
+    forwards = [
+        forward_of(part, away, other)
+        for other in range(side)
+        for away in range(1, side)
+        for part in range(2)
+    ]
+
+    sent_ref[...] = jnp.full_like(sent_ref, -1)
+    for t in range(shards):
+        in_bag = iota((BAG, mine), 0) < lengths_ref[t : t + 1, :]
+        sent_ref[t, 0:BAG, :mine] = idx_first_ref[t]
+        sent_ref[t, BAG : 2 * BAG, :mine] = idx_middle_ref[t]
+        sent_ref[t, 2 * BAG : 3 * BAG, :mine] = jnp.where(in_bag, idx_last_ref[t], -1)
+
+    def ids_of(i):
+        to = lax.rem(me + i, shards)
+        return pltpu.make_async_remote_copy(
+            src_ref=sent_ref.at[to], dst_ref=got_ref.at[me],
+            send_sem=ids_send.at[i], recv_sem=ids_recv.at[i],
+            device_id={"tables": to}, device_id_type=MESH,
+        )
+
+    pl.semaphore_wait(barrier, shards + replicas - 2)
+    for i in range(1, shards):
+        ids_of(i).start()
+    keep.wait()
+    for spread in spreads:
+        spread.start()
+    got_ref[me] = sent_ref[me]
 
     def make_pair(g, carry):
         core = middle_ref[pl.ds(g, 1)].reshape(rank, wide)
@@ -167,6 +216,29 @@
     swap = (to_lane == (from_row & (D3 - 1)) * rank + (from_row >> 3)).astype(F32).astype(BF16)
     last_by_d3_ref[...] = dot(last_ref[...], swap).astype(BF16)
 
+    taps = D2 * D3 * LANES
+    tap, spot = iota((taps, LANES), 0), iota((taps, LANES), 1)
+    gather_own_ref[...] = (spot == (tap & (D1 - 1)) * (D2 * D3) + (tap >> 7)).astype(F32).astype(BF16)
+
+    for i in range(1, shards):
+        ids_of(i).wait()
+    group_items(groups, got_ref, dest_v, owner_v, slot_ref, rank_ref, places_ref)
+    to_scalars = [
+        pltpu.make_async_copy(dest_v, dest_ref, weight_sem.at[3]),
+        pltpu.make_async_copy(owner_v, owner_ref, weight_sem.at[4]),
+    ]
+    for copy in to_scalars:
+        copy.start()
+    last_ids_ref[...] = jnp.transpose(
+        got_ref[...].reshape(shards * got_ref.shape[1], got_ref.shape[2]).astype(F32)
+    )
+    for spread in spreads:
+        spread.wait()
+    for forward in forwards:
+        forward.start()
+    for copy in to_scalars:
+        copy.wait()
+
     per_step = STEP // TILE
     pairs = left_ref.shape[0] // (2 * STEP)
     slot_lane = iota((LANES, LANES), 1)
@@ -185,7 +257,7 @@
 
     def make_left(step, from_ref):
         for t in range(per_step):
-            owner = owner_ref[0, step * per_step + t]
+            owner = jnp.clip(owner_ref[0, step * per_step + t], 0, groups - 1)
             stacked = jnp.concatenate(
                 [
                     from_ref[t * TILE : (t + 1) * TILE, p * LANES : (p + 1) * LANES]
@@ -217,32 +289,27 @@
     lax.fori_loop(0, pairs, left_pair, 0)
 
     group = TILE
-    unit = last_ids_ref.shape[0]
+    unit = diag_a_ref.shape[0]
     units = mine // unit
     per_unit = unit // group
-    id_lane = iota(last_ids_ref.shape, 1)
+    id_lane = iota((unit, LANES), 1)
     low_half = iota((group, LANES), 1) < rank
     own = (iota((group, LANES), 1) >> 3) == (iota((group, LANES), 0) & 15)
-    taps = D2 * D3 * LANES
-    tap, spot = iota((taps, LANES), 0), iota((taps, LANES), 1)
-    gather_own_ref[...] = (spot == (tap & (D1 - 1)) * (D2 * D3) + (tap >> 7)).astype(F32).astype(BF16)
-
-    def gather_last(number, to_ref):
-        hots = [
-            hot_of(
-                jnp.sum(
-                    jnp.where(id_lane == k * shards * units + number, last_ids_ref[...], 0), axis=1, keepdims=True
-                )
-            )
-            for k in range(BAG)
-        ]
+    def gather_last(source, number, to_ref):
+        rows_here = last_ids_ref[number * unit : (number + 1) * unit, :]
+        hots = []
+        for k in range(BAG):
+            mark = source * got_ref.shape[1] + 2 * BAG + k
+            ids = jnp.sum(jnp.where(id_lane == mark, rows_here, 0.0), axis=1, keepdims=True)
+            hots.append(hot_of(ids.astype(I32)))
         to_ref[...] = dot(jnp.concatenate(hots, axis=0), last_by_d3_ref[...])
 
-    def make_group(number, part, which, from_ref, diag_ref):
+    def make_group(source, number, part, from_ref, diag_ref):
         base = number * unit + part * group
+        which = number * per_unit + part
         for k in range(BAG):
             for q in range(group):
-                at = dest_ref[k * queries + base + q]
+                at = jnp.clip(dest_ref[k * shards + source, base + q], 0, left_ref.shape[0] - 1)
                 staged_ref[which, k, q] = left_ref[at]
         right = jnp.concatenate(
             [staged_ref[which, k].reshape(group * D1, wide) for k in range(BAG)], axis=1
@@ -271,7 +338,7 @@
 
     def make_unit(to, number, from_ref, diag_ref):
         for part in range(per_unit):
-            make_group(to * units + number, part, number * per_unit + part, from_ref, diag_ref)
+            make_group(to, number, part, from_ref, diag_ref)
         out_ref[to, number * unit : (number + 1) * unit, :] = dot(
             diag_ref[...], gather_own_ref[...]
         ).astype(BF16)
@@ -287,14 +354,13 @@
             device_id_type=MESH,
         )
 
-    gather_last(lax.rem(me + 1, shards) * units, last_a_ref)
-    pl.semaphore_wait(barrier, shards + replicas - 2)
+    gather_last(lax.rem(me + 1, shards), 0, last_a_ref)
 
     def make_owner(i, carry):
         to, after = lax.rem(me + 1 + i, shards), lax.rem(me + 2 + i, shards)
-        gather_last(to * units + 1, last_b_ref)
+        gather_last(to, 1, last_b_ref)
         make_unit(to, 0, last_a_ref, diag_a_ref)
-        gather_last(after * units, last_a_ref)
+        gather_last(after, 0, last_a_ref)
         make_unit(to, 1, last_b_ref, diag_b_ref)
 
         @pl.when(i < shards - 1)
@@ -304,6 +370,8 @@
         return carry
 
     lax.fori_loop(0, shards, make_owner, 0)
+    for forward in forwards:
+        forward.wait()
     fetches[2].start()
     recv_ref[me] = out_ref[me]
     for i in range(shards - 1):
@@ -329,16 +397,15 @@
         sum_ref[...] = jnp.zeros_like(sum_ref)
 
         def step(t, carry):
-            span = down_v.shape[1] // D1
             weight = jnp.concatenate(
                 [left_ref[pl.ds((2 * t + h) * span, span)].reshape(span * D1, lanes) for h in range(2)], axis=1
             )
             hidden = dot(rows_ref[...], weight)
             for half in range(2):
                 at = 2 * t + half
-                unit = hidden[:, half * lanes : (half + 1) * lanes] + top_bias_ref[pl.ds(at, 1), :]
+                unit = hidden[:, half * lanes : (half + 1) * lanes] + units_ref[pl.ds(2 * at + core, 1), :]
                 unit = jnp.maximum(unit, 0.0).astype(BF16).astype(F32)
-                sum_ref[:mine] += unit * out_weight_ref[pl.ds(at, 1), :]
+                sum_ref[:mine] += unit * units_ref[pl.ds(2 * (shards + at) + core, 1), :]
             return carry
 
         lax.fori_loop(0, shards // 2, step, 0)
@@ -380,27 +447,41 @@
 
 
 def main(
-    dest, owner, slot, last_ids, core_first, core_middle, core_last,
-    weight, cross_down, cross_up, cross_bias, top_bias, out_weight, prior,
+    idx_first, idx_middle, idx_last, lengths, core_first, core_middle, core_last,
+    top_weight, cross_down, cross_up, cross_bias, units, prior,
 ):
-    items = dest.size
     groups, rank, wide = core_middle.shape
-    slots = -(-(items + groups * TILE) // (2 * STEP)) * 2 * STEP
     shards, replicas = lax.axis_size("tables"), lax.axis_size("replica")
     queries = prior.shape[1]
-    feat = cross_down.shape[1]
+    items = shards * queries * BAG
+    slots = -(-(items + groups * TILE) // (2 * STEP)) * 2 * STEP
+    feat, hid = top_weight.shape
     padded = -(-queries // LANES) * LANES
-    unit = last_ids.shape[0]
-    smem = pl.BlockSpec(memory_space=pltpu.SMEM)
+    unit = queries // 2
+    owners = -(-(slots // TILE) // LANES) * LANES
+    side = 4 if shards == 16 else 1
     vmem = pl.BlockSpec(memory_space=pltpu.VMEM)
     anywhere = pl.BlockSpec(memory_space=pl.ANY)
     dma = pltpu.SemaphoreType.DMA
     return pl.pallas_call(
-        functools.partial(main_kernel, items),
-        out_shape=jax.ShapeDtypeStruct((2, queries), F32),
-        in_specs=[smem, smem, vmem, vmem, vmem, vmem, vmem, anywhere, anywhere, anywhere, vmem, vmem, vmem, vmem],
-        out_specs=vmem,
+        main_kernel,
+        out_shape=(
+            jax.ShapeDtypeStruct((2, queries), F32),
+            jax.ShapeDtypeStruct((shards * feat // D1, D1, LANES), BF16),
+        ),
+        in_specs=[vmem] * 7 + [anywhere] * 3 + [vmem] * 3,
+        out_specs=(vmem, anywhere),
         scratch_shapes=[
+            pltpu.VMEM((shards, 8, padded), I32),
+            pltpu.VMEM((shards, 8, padded), I32),
+            pltpu.VMEM((padded, shards * 8), F32),
+            pltpu.VMEM((BAG * shards, padded), I32),
+            pltpu.VMEM((8, owners), I32),
+            pltpu.VMEM((LANES, LANES), I32),
+            pltpu.VMEM((BAG * shards, padded), F32),
+            pltpu.VMEM((2 * LANES, LANES), F32),
+            pltpu.SMEM((BAG * shards, padded), I32),
+            pltpu.SMEM((8, owners), I32),
             pltpu.VMEM((groups, 2 * rank, 2 * wide), BF16),
             pltpu.VMEM(core_last.shape, BF16),
             pltpu.VMEM((slots, D1, wide), BF16),
@@ -425,7 +506,14 @@
             pltpu.VMEM((padded, LANES), F32),
             dma((shards,)),
             dma((shards,)),
-            dma((3,)),
+            dma((2, side)),
+            dma((2, side)),
+            dma((2, side, side)),
+            dma((2, side, side)),
+            dma,
+            dma((shards,)),
+            dma((shards,)),
+            dma((5,)),
             dma,
             dma,
             dma,
@@ -439,8 +527,8 @@
         cost_estimate=pl.CostEstimate(flops=int(100e9), bytes_accessed=24000000, transcendentals=0),
         name="main",
     )(
-        dest.reshape(-1), owner, slot, last_ids, core_first, core_middle, core_last,
-        weight.reshape(-1, D1, LANES), cross_down, cross_up, cross_bias, top_bias, out_weight, prior,
+        idx_first, idx_middle, idx_last, lengths, core_first, core_middle, core_last,
+        top_weight.reshape(feat // D1, D1, hid), cross_down, cross_up, cross_bias, units, prior,
     )
 
 
@@ -460,51 +548,23 @@
     out_weight,
     prior,
 ):
-    shards = lax.axis_size("tables")
-    queries = idx_first.shape[2]
-
-    core = lax.rem(lax.axis_index("replica"), 2)
-    half = top_weight.shape[1] // 2
-    part = lax.dynamic_slice_in_dim(top_weight, core * half, half, axis=1)
-    weight = lax.all_gather(part, "tables", axis=0)
-
-    def my_units(values):
-        return lax.dynamic_index_in_dim(values.reshape(shards, 2, half), core, 1, keepdims=False)
-
-    in_bag = jnp.arange(BAG, dtype=I32)[None, :, None] < bag_lengths[0, 0].T[:, None, :]
-
     def by_table(values):
         return jnp.transpose(values[0, 0], (1, 2, 0))
 
-    sent = jnp.concatenate(
-        [
-            by_table(idx_first),
-            by_table(idx_middle),
-            jnp.where(in_bag, by_table(idx_last), -1),
-        ],
-        axis=1,
-    )
-    at_owner = lax.all_to_all(sent, "tables", split_axis=0, concat_axis=0, tiled=True)
-    at_owner = jnp.transpose(at_owner, (1, 0, 2))
-    first_ids, middle_ids, last_ids = (
-        at_owner[BAG * i : BAG * (i + 1)].reshape(-1, LANES) for i in range(3)
-    )
-    dest, owner, slot = order(first_ids, middle_ids, core_middle.shape[1])
-    unit = queries // 2
-    both = main(
-        dest,
-        owner,
-        slot,
-        last_ids.reshape(-1, unit).T,
+    units = jnp.concatenate([top_bias, out_weight]).astype(F32).reshape(-1, LANES)
+    both, _ = main(
+        by_table(idx_first),
+        by_table(idx_middle),
+        by_table(idx_last),
+        bag_lengths[0, 0].T,
         core_first[0],
         core_middle[0],
         core_last[0],
-        weight,
+        top_weight,
         cross_down,
         cross_up,
         cross_bias,
-        my_units(top_bias).astype(F32),
-        my_units(out_weight).astype(F32),
+        units,
         prior[0],
     )
     return (both[:1][None], both[1:][None])

time: 174 us -> 133 us (0.76)
  waiting for transfers between devices: 53.6 us -> 0 us
  Pallas kernels: 87.4 us -> 130 us
  between operations: 14.1 us -> 0.64 us
  starting transfers between devices: 7.62 us -> 0 us
  local copies, waits for them, and re-layouts: 7.06 us -> 1.32 us
  other arithmetic: 3.6 us -> 1.33 us
    all_gather x1 -> x0, waiting for transfers between devices: 47.6 us -> none  [body(): weight = lax.all_gather(part, 'tables', axis=0)]
    pallas_call x2 -> x1, Pallas kernels: 87.4 us -> 130 us  [main(): pl.pallas_call(main_kernel, out_shape=(jax.ShapeDtypeStruct((2, queries),...]
    all_to_all x1 -> x0, starting transfers between devices: 7.58 us -> none  [body(): lax.all_to_all(sent, 'tables', split_axis=0, concat_axis=0, tiled=True)]
    all_to_all x1 -> x0, waiting for transfers between devices: 5.94 us -> none  [body(): lax.all_to_all(sent, 'tables', split_axis=0, concat_axis=0, tiled=True)]
    unnamed x7 -> x0, local copies, waits for them, and re-layouts: 2.57 us -> none
    another operation x4 -> x0, local copies, waits for them, and re-layouts: 2.21 us -> none  [the longest x2 0.81 us: body(): last_ids.reshape(-1, unit)]
  transfers between devices with their start and end apart: 2 -> 0, of which waited for: 2 -> 0; matrix products, arithmetic and copies ran while one was open for 4% -> 0% of each run, Pallas kernels for 4% -> 0%
where the time goes in v4:
time: 133 us
  Pallas kernels  130 us (98%)
  other arithmetic  1.33 us (1%)
    pallas_call x1, Pallas kernels, main(): pl.pallas_call(main_kernel, out_shape=(jax.ShapeDtypeStruct((2, queries),...  130 us

profile of v4, /device:TPU:1, one launch (start us, length us, event | category | flops | bytes accessed | tf_op | source)
XLA Modules:
  0.0 132.8 jit_solution(200254659167171346)
XLA Ops:
  0.6 1.3 %maximum_convert_fusion.units_ref = f32[64,128]{1,0:T(8,128)} fusion(bf16[32,128]{1,0:T(8,128)(2,1)} %bitcast.23, bf16[32,128]{1,0:T(8,128)(2,1)} %bitcast.24), kind=kLoop, calls=%fused_computation | loop fusion | flops 32768 | bytes 49152 | tf_op jit(solution)/shard_map/convert_element_type | solution.py:554
  2.0 129.5 %main.1 = (f32[2,320]{1,0:T(2,128)}, bf16[4096,8,128]{2,1,0:T(8,128)(2,1)}) custom-call(s32[16,2,320]{2,1,0:T(2,128)} %bitcast.29, s32[16,2,320]{2,1,0:T(2,128)} %bitcast.30, s32[16,2,320]{2,1,0:T(2,128)} %bitcast.31, s32[16,320]{1,0:T(8,128)} %bitcast.32, bf16[512,512]{1,0:T(8,128)(2,1)} %bitcast.27, bf16[80,64,128]{2,1,0:T(8,128)(2,1)} %bitcast.25, ...), custom_call_target="tpu_custom_call" | custom-call | flops 99999997952 | bytes 24000000 | tf_op jit(solution)/shard_map/main/pallas_call | solution.py:466
  131.5 1.3 slice_bitcast_fusion

commit v5 on v4

--- a/solution.py
+++ b/solution.py
@@ -31,7 +31,7 @@
     return lax.dot_general(a, b, (((1,), (1,)), ((), ())), preferred_element_type=F32)
 
 
-def group_items(groups, got_ref, dest_ref, owner_ref, slot_ref, rank_ref, sums_ref):
+def group_items(groups, slots, got_ref, dest_ref, owner_ref, slot_ref, rank_ref, sums_ref):
     sources, _, width = got_ref.shape
     group_row = iota((groups, width), 0)
     lane_row = iota((LANES, width), 0)
@@ -70,9 +70,8 @@
     offset = 16.0 * dot(above, high.astype(BF16)) + dot(above, low.astype(BF16))
     offset = offset[:, :1]
     tile_lane = iota((groups, owner_ref.shape[1]), 1)
-    owner_ref[...] = jnp.broadcast_to(
-        jnp.sum((offset.astype(I32) <= tile_lane).astype(I32), axis=0, keepdims=True) - 1, owner_ref.shape
-    )
+    reached = jnp.sum((offset.astype(I32) <= tile_lane).astype(I32), axis=0, keepdims=True)
+    owner_ref[...] = jnp.broadcast_to(jnp.clip(reached - 1, 0, groups - 1), owner_ref.shape)
     sums_ref[...] = jnp.zeros_like(sums_ref)
 
     def place(step, carry):
@@ -81,7 +80,7 @@
         starts = [jnp.sum(jnp.where(group_row == row, offset, 0.0), axis=0, keepdims=True) for row in middles]
         dests = (rank_ref[pl.ds(first, together), :] + TILE * jnp.concatenate(starts, axis=0)).astype(I32)
         dests = jnp.where(jnp.concatenate(middles, axis=0) < 0, -1, dests)
-        dest_ref[pl.ds(first, together), :] = dests
+        dest_ref[pl.ds(first, together), :] = jnp.clip(dests, 0, slots - 1)
         ids = jnp.concatenate(rows_of(step, 0), axis=0)
         lanes, highs, lows, rows = dests & (LANES - 1), (ids >> 4).astype(F32), (ids & 15).astype(F32), dests >> 7
         values, spots = [], []
@@ -140,43 +139,71 @@
     fetches[0].start()
     fetches[1].start()
 
-    own_weight = top_ref.at[:, :, pl.ds(pl.multiple_of(core * lanes, lanes), lanes)]
-    half = span // 2
-
-    def shard_part(shard, part):
-        return weight_ref.at[pl.ds(shard * span + part * half, half)]
-
-    keep = pltpu.make_async_copy(own_weight, weight_ref.at[pl.ds(me * span, span)], local_sem)
+    rows_of_part = span // 2
+    keep = pltpu.make_async_copy(
+        top_ref.at[:, :, pl.ds(pl.multiple_of(core * lanes, lanes), lanes)],
+        weight_ref.at[pl.ds(me * span, span)],
+        local_sem,
+    )
     keep.start()
 
-    def spread_of(part, away):
-        to = row * side + lax.rem(column + away, side) if part == 0 else lax.rem(row + away, side) * side + column
+    def place_of(part, along, across):
+        u, v = (column, row) if part == 0 else (row, column)
+        u, v = lax.rem(u + along + side, side), lax.rem(v + across + side, side)
+        return v * side + u if part == 0 else u * side + v
+
+    def hop(part, shard, to, piece, mine_too, sems, at):
+        start, count = part * rows_of_part, rows_of_part
+        if piece is not None:
+            count = rows_of_part // 2
+            start = start + piece * count
+        dst = weight_ref.at[pl.ds(shard * span + start, count)]
+        src = dst
+        if mine_too:
+            src = top_ref.at[pl.ds(start, count), :, pl.ds(pl.multiple_of(core * lanes, lanes), lanes)]
         return pltpu.make_async_remote_copy(
-            src_ref=shard_part(me, part), dst_ref=shard_part(me, part),
-            send_sem=spread_send.at[part, away], recv_sem=spread_recv.at[part, away],
+            src_ref=src, dst_ref=dst, send_sem=sems[0].at[at], recv_sem=sems[1].at[at],
             device_id={"tables": to}, device_id_type=MESH,
         )
 
-    def forward_of(part, away, other):
-        if part == 0:
-            shard = row * side + lax.rem(column + other, side)
-            to = lax.rem(row + away, side) * side + column
-        else:
-            shard = lax.rem(row + other, side) * side + column
-            to = row * side + lax.rem(column + away, side)
-        return pltpu.make_async_remote_copy(
-            src_ref=shard_part(shard, part), dst_ref=shard_part(shard, part),
-            send_sem=forward_send.at[part, away, other], recv_sem=forward_recv.at[part, away, other],
-            device_id={"tables": to}, device_id_type=MESH,
-        )
-
-    spreads = [spread_of(part, away) for away in range(1, side) for part in range(2)]
-    forwards = [
-        forward_of(part, away, other)
-        for other in range(side)
-        for away in range(1, side)
-        for part in range(2)
-    ]
+    ways = [(part, way, 1 - 2 * way) for part in range(2) for way in range(2)]
+
+    def spread():
+        return [
+            hop(p, me, place_of(p, d, 0), None, True, (spread_send, spread_recv), (p, w, 0)) for p, w, d in ways
+        ]
+
+    def spread_on():
+        return [
+            hop(p, place_of(p, -d, 0), place_of(p, d, 0), w, False, (spread_send, spread_recv), (p, w, 1))
+            for p, w, d in ways
+        ]
+
+    def forward(others):
+        return [
+            hop(
+                p, place_of(p, j, 0), place_of(p, 0, d), None, j == 0, (forward_send, forward_recv), (p, w, 0, j)
+            )
+            for j in others
+            for p, w, d in ways
+        ]
+
+    def forward_on(others):
+        return [
+            hop(
+                p, place_of(p, j, -d), place_of(p, 0, d), w, False, (forward_send, forward_recv), (p, w, 1, j)
+            )
+            for j in others
+            for p, w, d in ways
+        ]
+
+    def start(copies):
+        for copy in copies:
+            copy.start()
+
+    def wait(copies):
+        for copy in copies:
+            copy.wait()
 
     sent_ref[...] = jnp.full_like(sent_ref, -1)
     for t in range(shards):
@@ -196,9 +223,8 @@
     pl.semaphore_wait(barrier, shards + replicas - 2)
     for i in range(1, shards):
         ids_of(i).start()
-    keep.wait()
-    for spread in spreads:
-        spread.start()
+    start(spread())
+    start(forward([0]))
     got_ref[me] = sent_ref[me]
 
     def make_pair(g, carry):
@@ -222,7 +248,7 @@
 
     for i in range(1, shards):
         ids_of(i).wait()
-    group_items(groups, got_ref, dest_v, owner_v, slot_ref, rank_ref, places_ref)
+    group_items(groups, left_ref.shape[0], got_ref, dest_v, owner_v, slot_ref, rank_ref, places_ref)
     to_scalars = [
         pltpu.make_async_copy(dest_v, dest_ref, weight_sem.at[3]),
         pltpu.make_async_copy(owner_v, owner_ref, weight_sem.at[4]),
@@ -232,10 +258,11 @@
     last_ids_ref[...] = jnp.transpose(
         got_ref[...].reshape(shards * got_ref.shape[1], got_ref.shape[2]).astype(F32)
     )
-    for spread in spreads:
-        spread.wait()
-    for forward in forwards:
-        forward.start()
+    wait(spread())
+    start(spread_on())
+    start(forward([1, 3]))
+    wait(forward([0]))
+    start(forward_on([0]))
     for copy in to_scalars:
         copy.wait()
 
@@ -280,6 +307,13 @@
     gather_first(0, cores_a_ref)
 
     def left_pair(pair, carry):
+        @pl.when(pair == pairs // 2)
+        def _():
+            wait(spread_on())
+            start(forward([2]))
+            wait(forward([1, 3]))
+            start(forward_on([1, 3]))
+
         gather_first(2 * pair + 1, cores_b_ref)
         make_left(2 * pair, cores_a_ref)
         gather_first(2 * pair + 2, cores_a_ref)
@@ -309,7 +343,7 @@
         which = number * per_unit + part
         for k in range(BAG):
             for q in range(group):
-                at = jnp.clip(dest_ref[k * shards + source, base + q], 0, left_ref.shape[0] - 1)
+                at = dest_ref[k * shards + source, base + q]
                 staged_ref[which, k, q] = left_ref[at]
         right = jnp.concatenate(
             [staged_ref[which, k].reshape(group * D1, wide) for k in range(BAG)], axis=1
@@ -357,6 +391,11 @@
     gather_last(lax.rem(me + 1, shards), 0, last_a_ref)
 
     def make_owner(i, carry):
+        @pl.when(i == 3)
+        def _():
+            wait(forward([2]))
+            start(forward_on([2]))
+
         to, after = lax.rem(me + 1 + i, shards), lax.rem(me + 2 + i, shards)
         gather_last(to, 1, last_b_ref)
         make_unit(to, 0, last_a_ref, diag_a_ref)
@@ -370,8 +409,8 @@
         return carry
 
     lax.fori_loop(0, shards, make_owner, 0)
-    for forward in forwards:
-        forward.wait()
+    keep.wait()
+    wait(forward_on([0, 1, 3, 2]))
     fetches[2].start()
     recv_ref[me] = out_ref[me]
     for i in range(shards - 1):
@@ -393,32 +432,38 @@
     pair.start()
     fetches[2].wait()
 
-    def summed(rows_ref):
-        sum_ref[...] = jnp.zeros_like(sum_ref)
-
+    def add_units(rows_ref, to_ref, begin, end):
         def step(t, carry):
             weight = jnp.concatenate(
                 [left_ref[pl.ds((2 * t + h) * span, span)].reshape(span * D1, lanes) for h in range(2)], axis=1
             )
             hidden = dot(rows_ref[...], weight)
-            for half in range(2):
-                at = 2 * t + half
-                unit = hidden[:, half * lanes : (half + 1) * lanes] + units_ref[pl.ds(2 * at + core, 1), :]
+            for h in range(2):
+                at = 2 * t + h
+                unit = hidden[:, h * lanes : (h + 1) * lanes] + units_ref[pl.ds(2 * at + core, 1), :]
                 unit = jnp.maximum(unit, 0.0).astype(BF16).astype(F32)
-                sum_ref[:mine] += unit * units_ref[pl.ds(2 * (shards + at) + core, 1), :]
+                to_ref[:mine] += unit * units_ref[pl.ds(2 * (shards + at) + core, 1), :]
             return carry
 
-        lax.fori_loop(0, shards // 2, step, 0)
-        return jnp.sum(jnp.transpose(sum_ref[...]), axis=0, keepdims=True)
-
-    ours = summed(mine_ref)
+        lax.fori_loop(begin, end, step, 0)
+
+    def as_row(from_ref):
+        return jnp.sum(jnp.transpose(from_ref[...]), axis=0, keepdims=True)
+
+    ours_ref, their_sum_ref = sum_ref.at[0], sum_ref.at[1]
+    sum_ref[...] = jnp.zeros_like(sum_ref)
+    steps = shards // 2
+    add_units(mine_ref, ours_ref, 0, steps // 2)
     pair.wait()
-    part_ref[...] = jnp.broadcast_to(summed(theirs_ref), part_ref.shape)
+    add_units(theirs_ref, their_sum_ref, 0, steps)
+    part_ref[...] = jnp.broadcast_to(as_row(their_sum_ref), part_ref.shape)
     back = pltpu.make_async_remote_copy(
         src_ref=part_ref, dst_ref=part_in_ref, send_sem=part_send, recv_sem=part_recv,
         device_id={"replica": sibling}, device_id_type=MESH,
     )
     back.start()
+    add_units(mine_ref, ours_ref, steps // 2, steps)
+    ours = as_row(ours_ref)
     back.wait()
     logits = (ours + part_in_ref[:1])[:, :mine] + prior_ref[...]
     both_ref[:1] = logits
@@ -503,13 +548,13 @@
             pltpu.VMEM((8, padded), F32),
             pltpu.VMEM((8, padded), F32),
             pltpu.VMEM((replicas, 8, LANES), F32),
-            pltpu.VMEM((padded, LANES), F32),
+            pltpu.VMEM((2, padded, LANES), F32),
             dma((shards,)),
             dma((shards,)),
-            dma((2, side)),
-            dma((2, side)),
-            dma((2, side, side)),
-            dma((2, side, side)),
+            dma((2, 2, 2)),
+            dma((2, 2, 2)),
+            dma((2, 2, 2, side)),
+            dma((2, 2, 2, side)),
             dma,
             dma((shards,)),
             dma((shards,)),

time: 133 us -> 112 us (0.84)
  Pallas kernels: 130 us -> 109 us
    pallas_call x1, Pallas kernels: 130 us -> 109 us  [main(): pl.pallas_call(main_kernel, out_shape=(jax.ShapeDtypeStruct((2, queries),...]
where the time goes in v5:
time: 112 us
  Pallas kernels  109 us (97%)
  other arithmetic  1.33 us (1%)
  local copies, waits for them, and re-layouts  1.32 us (1%)
    pallas_call x1, Pallas kernels, main(): pl.pallas_call(main_kernel, out_shape=(jax.ShapeDtypeStruct((2, queries),...  109 us

profile of v5, /device:TPU:1, one launch (start us, length us, event | category | flops | bytes accessed | tf_op | source)
XLA Modules:
  0.0 112.1 jit_solution(14064944256214089921)
XLA Ops:
  0.6 1.3 %maximum_convert_fusion.units_ref = f32[64,128]{1,0:T(8,128)} fusion(bf16[32,128]{1,0:T(8,128)(2,1)} %bitcast.23, bf16[32,128]{1,0:T(8,128)(2,1)} %bitcast.24), kind=kLoop, calls=%fused_computation | loop fusion | flops 32768 | bytes 49152 | tf_op jit(solution)/shard_map/convert_element_type | solution.py:599
  2.0 108.8 %main.1 = (f32[2,320]{1,0:T(2,128)}, bf16[4096,8,128]{2,1,0:T(8,128)(2,1)}) custom-call(s32[16,2,320]{2,1,0:T(2,128)} %bitcast.29, s32[16,2,320]{2,1,0:T(2,128)} %bitcast.30, s32[16,2,320]{2,1,0:T(2,128)} %bitcast.31, s32[16,320]{1,0:T(8,128)} %bitcast.32, bf16[512,512]{1,0:T(8,128)(2,1)} %bitcast.27, bf16[80,64,128]{2,1,0:T(8,128)(2,1)} %bitcast.25, ...), custom_call_target="tpu_custom_call" | custom-call | flops 99999997952 | bytes 24000000 | tf_op jit(solution)/shard_map/main/pallas_call | solution.py:511
  110.8 1.3 %slice_bitcast_fusion = (f32[1,1,320]{2,1,0:T(1,128)}, f32[1,1,320]{2,1,0:T(1,128)}) fusion(f32[2,320]{1,0:T(2,128)} %get-tuple-element.3), kind=kLoop, calls=%fused_computation.1 | loop fusion | bytes 5120 | tf_op jit(solution)/shard_map/broadcast_in_dim | solution.py:615

commit v6 on v5

--- a/solution.py
+++ b/solution.py
@@ -267,7 +267,8 @@
         copy.wait()
 
     per_step = STEP // TILE
-    pairs = left_ref.shape[0] // (2 * STEP)
+    steps_left = left_ref.shape[0] // STEP
+    pairs = steps_left // 2
     slot_lane = iota((LANES, LANES), 1)
 
     def hot_of(ids):
@@ -321,6 +322,8 @@
         return carry
 
     lax.fori_loop(0, pairs, left_pair, 0)
+    if steps_left % 2:
+        make_left(steps_left - 1, cores_a_ref)
 
     group = TILE
     unit = diag_a_ref.shape[0]
@@ -499,7 +502,7 @@
     shards, replicas = lax.axis_size("tables"), lax.axis_size("replica")
     queries = prior.shape[1]
     items = shards * queries * BAG
-    slots = -(-(items + groups * TILE) // (2 * STEP)) * 2 * STEP
+    slots = -(-(items + groups * TILE) // STEP) * STEP
     feat, hid = top_weight.shape
     padded = -(-queries // LANES) * LANES
     unit = queries // 2

time: 112 us -> 111 us (level)
    pallas_call x1, Pallas kernels: 109 us -> 108 us  [main(): pl.pallas_call(main_kernel, out_shape=(jax.ShapeDtypeStruct((2, queries),...]
where the time goes in v6:
time: 111 us
  Pallas kernels  108 us (97%)
  other arithmetic  1.33 us (1%)
  local copies, waits for them, and re-layouts  1.32 us (1%)
    pallas_call x1, Pallas kernels, main(): pl.pallas_call(main_kernel, out_shape=(jax.ShapeDtypeStruct((2, queries),...  108 us

profile of v6, /device:TPU:1, one launch (start us, length us, event | category | flops | bytes accessed | tf_op | source)
XLA Modules:
  0.0 110.9 jit_solution(999810064254364885)
XLA Ops:
  0.6 1.3 %maximum_convert_fusion.units_ref = f32[64,128]{1,0:T(8,128)} fusion(bf16[32,128]{1,0:T(8,128)(2,1)} %bitcast.23, bf16[32,128]{1,0:T(8,128)(2,1)} %bitcast.24), kind=kLoop, calls=%fused_computation | loop fusion | flops 32768 | bytes 49152 | tf_op jit(solution)/shard_map/convert_element_type | solution.py:602
  2.0 107.6 %main.1 = (f32[2,320]{1,0:T(2,128)}, bf16[4096,8,128]{2,1,0:T(8,128)(2,1)}) custom-call(s32[16,2,320]{2,1,0:T(2,128)} %bitcast.29, s32[16,2,320]{2,1,0:T(2,128)} %bitcast.30, s32[16,2,320]{2,1,0:T(2,128)} %bitcast.31, s32[16,320]{1,0:T(8,128)} %bitcast.32, bf16[512,512]{1,0:T(8,128)(2,1)} %bitcast.27, bf16[80,64,128]{2,1,0:T(8,128)(2,1)} %bitcast.25, ...), custom_call_target="tpu_custom_call" | custom-call | flops 99999997952 | bytes 24000000 | tf_op jit(solution)/shard_map/main/pallas_call | solution.py:514
  109.6 1.3 %slice_bitcast_fusion = (f32[1,1,320]{2,1,0:T(1,128)}, f32[1,1,320]{2,1,0:T(1,128)}) fusion(f32[2,320]{1,0:T(2,128)} %get-tuple-element.3), kind=kLoop, calls=%fused_computation.1 | loop fusion | bytes 5120 | tf_op jit(solution)/shard_map/broadcast_in_dim | solution.py:618
